TPU v7x, 32 devices: a whole 2x2x4 slice. The times are simulated.
32 devices in a mesh: section: 2 (over core), row: 16 (over z, y, x).
Axes of the slice: x: 2, y: 2, z: 4, core: 2. Of those that a mesh axis runs over, the one named last changes fastest.
Arguments:
- tokens: bfloat16 [2, 8192, 384], P(None, 'row'), may hold values from -3 to 3
- conditions: bfloat16 [2, 32, 384], P(None, 'row'), may hold values from -2.5 to 2.5
- output_grad: bfloat16 [2, 8192, 384], P(None, 'row'), may hold values from -3 to 3
- layouts: int32 [2, 16], P(None, 'row'), may hold values from 0 to 2
- w_ada: bfloat16 [2, 384, 2304], P('section', 'row'), may hold values from -0.3125 to 0.3125
- b_ada: float32 [2, 2304], P('section'), may hold values from -0.5 to 0.5
- w_query: bfloat16 [2, 384, 384], P('section', 'row'), may hold values from -0.3125 to 0.3125
- w_key: bfloat16 [2, 384, 384], P('section', 'row'), may hold values from -0.3125 to 0.3125
- w_value: bfloat16 [2, 384, 384], P('section', 'row'), may hold values from -0.3125 to 0.3125
- w_gate: bfloat16 [2, 384, 384], P('section', 'row'), may hold values from -0.3125 to 0.3125
- w_out: bfloat16 [2, 384, 384], P('section', 'row'), may hold values from -0.4375 to 0.4375
- w_decay: bfloat16 [2, 384, 6], P('section', 'row'), may hold values from -0.3125 to 0.3125
- b_decay: float32 [2, 6], P('section'), may hold values from -3 to 6
- conv_kernel: float32 [2, 3, 384], P('section'), may hold values from -3 to 3
- w_up: bfloat16 [2, 384, 1536], P('section', 'row'), may hold values from -0.3125 to 0.3125
- b_up: float32 [2, 1536], P('section'), may hold values from -2 to 2
- w_down: bfloat16 [2, 1536, 384], P('section', 'row'), may hold values from -0.15625 to 0.15625
- b_down: float32 [2, 384], P('section'), may hold values from -2 to 2
Outputs:
- activations: bfloat16 [2, 2, 8192, 384], P('section', None, 'row')
- input_grads: float32 [2, 2, 8192, 384], P('section', None, 'row')
- cond_grads: float32 [2, 32, 384], P(None, 'row')
- grad_w_ada: float32 [2, 384, 2304], P('section', 'row')
- grad_b_ada: float32 [2, 2304], P('section')
- grad_w_query: float32 [2, 384, 384], P('section', 'row')
- grad_w_key: float32 [2, 384, 384], P('section', 'row')
- grad_w_value: float32 [2, 384, 384], P('section', 'row')
- grad_w_gate: float32 [2, 384, 384], P('section', 'row')
- grad_w_out: float32 [2, 384, 384], P('section', 'row')
- grad_w_decay: float32 [2, 384, 6], P('section', 'row')
- grad_b_decay: float32 [2, 6], P('section')
- grad_conv_kernel: float32 [2, 3, 384], P('section')
- grad_w_up: float32 [2, 384, 1536], P('section', 'row')
- grad_b_up: float32 [2, 1536], P('section')
- grad_w_down: float32 [2, 1536, 384], P('section', 'row')
- grad_b_down: float32 [2, 384], P('section')
Inputs may be any that keep to these rules, and one draw needn't show every extreme that they name: `layouts`: 0: the block of 512 rows holds one item of 16 x 32 patches; k: k items of 16 x 16 patches followed by empty rows.
All inputs are finite; a program needn't handle non-finite values.
Results may differ from a plain program's by a relative error of at most 0.018.
The roundings to bfloat16 on the way count: a program that leaves them out, or rounds other values in their place, can miss the bound.
Values may be sent and summed in bfloat16 or wider, within the bound.
No kernel may reach another device: no remote copies, remote signals or barrier semaphores. Data moves between devices by JAX's collectives and lax.ppermute only.
A program may use at most 256 MiB of HBM per device.

v0:
```python
import functools

import jax
import jax.numpy as jnp
from jax import lax
from jax.experimental import pallas as pl
from jax.experimental.pallas import tpu as pltpu
from jax.sharding import PartitionSpec as P

D = 384
HEADS = 6
HEAD_DIM = 64
FF = 1536
MICRO = 2
ROWS = 512
HALF = 256
SLOTS = 2
PAIR = 128
PAIRS = D // PAIR
QKVG = 4 * D
LANES = 128
GROUP = (QKVG + D + LANES) // 2
NEG = -1e30
SCALE = HEAD_DIM**-0.5

bf16 = jnp.bfloat16
f32 = jnp.float32


def mm(left, right):
    return jnp.dot(left, right, preferred_element_type=f32)


def mm_t(left, right):
    return lax.dot_general(left, right, (((1,), (1,)), ((), ())), preferred_element_type=f32)


def split(values):
    high = values.astype(bf16)
    return high, (values - high.astype(f32)).astype(bf16)


def split_three(values):
    high, rest = split(values)
    mid = values - high.astype(f32)
    middle, low = split(mid)
    return high, middle, low


def cat_left(values):
    high, low = split(values)
    return jnp.concatenate([high, low, high], axis=1)


def cat_right(values):
    high, low = split(values)
    return jnp.concatenate([high, high, low], axis=1)


def mm_near(left, right_pair, right_high):
    high, low = split(left)
    wide = mm(high, right_pair)
    return wide[:, :PAIR] + wide[:, PAIR:] + mm(low, right_high)


def lane_iota(rows, columns):
    return lax.broadcasted_iota(jnp.int32, (rows, columns), 1)


def row_iota(rows, columns):
    return lax.broadcasted_iota(jnp.int32, (rows, columns), 0)


def order_matrix(start, rows, wide, to_scan):
    t = row_iota(rows, ROWS) + start
    small = (t & 256) + ((t & 15) << 4) + ((t & 255) >> 4)
    if to_scan:
        large = ((t & 15) << 5) + (t >> 4)
    else:
        large = ((t & 31) << 4) + (t >> 5)
    source = jnp.where(wide, large, small)
    return jnp.where(lane_iota(rows, ROWS) == source, 1.0, 0.0).astype(bf16)


def normalise(values):
    centred = values - jnp.mean(values, axis=-1, keepdims=True)
    rate = lax.rsqrt(jnp.mean(centred * centred, axis=-1, keepdims=True) + 1e-06)
    return centred * rate, rate


def normalise_back(normal, rate, grad):
    return rate * (
        grad
        - jnp.mean(grad, axis=-1, keepdims=True)
        - normal * jnp.mean(grad * normal, axis=-1, keepdims=True)
    )


class In:
    def __init__(self, copy, kept):
        self.copy = copy
        self.kept = kept

    def __call__(self):
        if self.copy is not None:
            self.copy.wait()
            self.copy = None
        return self.kept


class Kernel:
    def __init__(self, layer, layouts):
        self.layer = layer
        self.section = lax.axis_index("section")
        self.own = self.section == layer
        self.layout = layouts[self.section, 0]
        self.wide = self.layout == 0
        self.live_rows = jnp.where(self.wide, ROWS, self.layout * HALF)
        self.pushed = {}

    def load(self, kind, refs, kept, sem):
        if kind == "own":
            mine, other = refs

            @pl.when(self.own)
            def _():
                pltpu.make_async_copy(mine, kept, sem).start()

            @pl.when(jnp.logical_not(self.own))
            def _():
                pltpu.make_async_copy(other, kept, sem).start()

            return In(pltpu.make_async_copy(mine, kept, sem), kept)
        (source,) = refs
        if kind == "micro":
            source = source.at[self.section if source.shape[0] == MICRO else 0]
        copy = pltpu.make_async_copy(source, kept, sem)
        copy.start()
        return In(copy, kept)

    def push(self, name):
        kept, target, sem = self.results[name]
        copy = pltpu.make_async_copy(kept, target, sem)
        copy.start()
        self.pushed[name] = copy

    def finish(self):
        for name in self.results:
            if name not in self.pushed:
                self.push(name)
        for copy in self.pushed.values():
            copy.wait()

    def slot(self, half):
        return jnp.where(self.wide, 0, half)

    def share(self, slot, part):
        row = pl.ds(2 * self.section + slot, 1)
        return self.mods()[row, part * D : (part + 1) * D]

    def bu(self):
        return self.small()[0:1, :]

    def bn(self):
        return self.small()[1:2, :D]

    def ck(self, tap):
        return self.small()[2 + tap : 3 + tap, :D]

    def bd(self):
        return self.small()[5:6, :LANES]


def sigmoid(values):
    return 1.0 / (1.0 + jnp.exp(-values))


GELU_A = 0.7978845608028654
GELU_B = 0.044715


def gelu_parts(values):
    square = values * values
    tanh = jnp.tanh(GELU_A * values * (1.0 + GELU_B * square))
    return square, tanh


def fill_bias(bias, wide):
    bias[:, :HALF] = jnp.full((HALF, HALF), 0.0, f32) + jnp.where(wide, 0.0, NEG)
    causal = row_iota(HALF, HALF) >= lane_iota(HALF, HALF)
    bias[:, HALF:] = jnp.where(causal, 0.0, NEG)


def decay_factors(cum, cumt, bias, head):
    row = cumt[pl.ds(head, 1), :]
    lanes = lane_iota(1, LANES)
    column = jnp.sum(jnp.where(lanes == head, cum[...], 0.0), axis=1, keepdims=True)
    first = jnp.exp(column[:HALF] - row[:, :HALF] + bias[:, HALF:])
    second = jnp.exp(column[HALF:] - row + bias[...])
    return first, second


def head_norm(values, lanes):
    square = values * values
    low = jnp.sum(jnp.where(lanes < HEAD_DIM, square, 0.0), axis=1, keepdims=True)
    high = jnp.sum(jnp.where(lanes < HEAD_DIM, 0.0, square), axis=1, keepdims=True)
    return jnp.where(lanes < HEAD_DIM, low, high) * (1.0 / HEAD_DIM)


def fill_decay(dp, bd, cum, cumt):
    raw = dp[...] + bd
    log_decay = (jnp.minimum(raw, 0.0) - jnp.log1p(jnp.exp(-jnp.abs(raw)))) * (1.0 / 16.0)
    high, middle, low = split_three(log_decay)
    causal = jnp.where(row_iota(ROWS, ROWS) >= lane_iota(ROWS, ROWS), 1.0, 0.0).astype(bf16)
    cum[...] = mm(causal, high) + mm(causal, middle) + mm(causal, low)
    cumt[...] = jnp.transpose(cum[...])


def columns(index, first=0):
    return pl.ds(pl.multiple_of(index * PAIR + first, PAIR), PAIR)


def attn_forward_body(k):
    flip = k.layer == 1
    wide = k.wide
    x = k.x()
    k.mods()

    def first(i, carry):
        rows = pl.ds(pl.multiple_of(i * HALF, HALF), HALF)
        slot = k.slot(i)
        normal, _ = normalise(x[rows, :].astype(f32))
        k.inner[rows, :] = (normal * (1.0 + k.share(slot, 1)) + k.share(slot, 0)).astype(bf16)
        return carry

    lax.fori_loop(0, 2, first, 0)
    w_qk = k.w_qk()
    w_vgd = k.w_vgd()

    def project(i, carry):
        start = pl.multiple_of(i * HALF, HALF)
        rows = pl.ds(start, HALF)
        if flip:
            part = mm(order_matrix(start, HALF, wide, True), k.inner[...]).astype(bf16)
        else:
            part = k.inner[rows, :]
        k.ordered[rows, :] = part
        k.qkvg[rows, : 2 * D] = mm(part, w_qk[...])
        k.qkvg[rows, 2 * D :] = mm(part, w_vgd[:, : 2 * D])
        k.dp[rows, :] = mm(part, w_vgd[:, 2 * D :])
        return carry

    lax.fori_loop(0, 2, project, 0)
    k.small()
    for name in ("ordered", "qkvg", "dp"):
        k.push(name)
    fill_decay(k.dp, k.bd(), k.cum, k.cumt)
    fill_bias(k.bias, wide)

    vpad = k.vpad
    vpad[0:8, :] = jnp.zeros((8, D), f32)
    vpad[8 : 8 + ROWS, :] = k.qkvg[:, 2 * D : 3 * D]
    position = row_iota(ROWS, 1) & jnp.where(wide, ROWS - 1, HALF - 1)
    one = jnp.where(position >= 1, vpad[7 : 7 + ROWS, :], 0.0)
    two = jnp.where(position >= 2, vpad[6 : 6 + ROWS, :], 0.0)
    k.vc[...] = k.ck(0) * vpad[8 : 8 + ROWS, :] + k.ck(1) * one + k.ck(2) * two
    for name in ("cum", "cumt", "vc"):
        k.push(name)

    def pair(p, carry):
        lanes = lane_iota(1, PAIR)
        queries = cat_left(k.qkvg[:, columns(p)] * SCALE)
        keys = k.qkvg[:, columns(p, D)]
        value_high, value_low = split(k.vc[:, columns(p)])
        values = jnp.concatenate([value_high, value_low], axis=1)
        parts = []
        for e in range(2):
            key_cat = cat_right(jnp.where((lanes // HEAD_DIM) == e, keys, 0.0))
            first, second = decay_factors(k.cum, k.cumt, k.bias, 2 * p + e)
            first = first * mm_t(queries[:HALF], key_cat[:HALF])
            second = second * mm_t(queries[HALF:], key_cat)
            parts.append(
                jnp.concatenate(
                    [
                        mm_near(first, values[:HALF], value_high[:HALF]),
                        mm_near(second, values, value_high),
                    ],
                    axis=0,
                )
            )
        total = jnp.where(lanes < HEAD_DIM, parts[0], parts[1])
        k.o[:, columns(p)] = total
        gate = k.qkvg[:, columns(p, 3 * D)]
        normed = total * lax.rsqrt(head_norm(total, lanes) + 1.0)
        mixed = (normed * (gate * sigmoid(gate))).astype(bf16)
        if flip:
            k.inner[:, columns(p)] = mixed
        else:
            k.gated[:, columns(p)] = mixed
        return carry

    lax.fori_loop(0, PAIRS, pair, 0)
    k.push("o")
    if flip:

        def back(i, carry):
            start = pl.multiple_of(i * HALF, HALF)
            k.gated[pl.ds(start, HALF), :] = mm(
                order_matrix(start, HALF, wide, False), k.inner[...]
            ).astype(bf16)
            return carry

        lax.fori_loop(0, 2, back, 0)


def ffn_forward_body(k):
    gated, x, wo = k.gated(), k.x(), k.wo()
    k.mods(), k.small()
    wu, wn = k.wu(), k.wn()

    def tile(i, carry):
        start = pl.multiple_of(i * HALF, HALF)
        rows = pl.ds(start, HALF)
        slot = k.slot(i)
        grown = mm(gated[rows, :], wo[...])
        k.branch[rows, :] = grown
        middle = x[rows, :].astype(f32) + k.share(slot, 2) * grown
        normal, _ = normalise(middle)
        inner = (normal * (1.0 + k.share(slot, 4)) + k.share(slot, 3)).astype(bf16)
        up = mm(inner, wu[...]) + k.bu()
        _, tanh = gelu_parts(up)
        hidden = (0.5 * up * (1.0 + tanh)).astype(bf16)
        low = mm(hidden, wn[...])
        k.down[rows, :] = low
        result = middle + k.share(slot, 5) * (low + k.bn())
        live = (row_iota(HALF, 1) + start) < k.live_rows
        k.out[rows, :] = jnp.where(live, result, 0.0).astype(bf16)
        return carry

    lax.fori_loop(0, 2, tile, 0)


def ffn_backward_body(k):
    gmod, gbu, gbn = k.gmod, k.gbu, k.gbn
    gmod[...] = jnp.zeros(gmod.shape, f32)
    gbu[...] = jnp.zeros(gbu.shape, f32)
    gbn[...] = jnp.zeros(gbn.shape, f32)
    k.mods(), k.small()
    x, grad, branch, down = k.x(), k.grad(), k.branch(), k.down()
    wu, wn = k.wu(), k.wn()

    def tile(i, carry):
        start = pl.multiple_of(i * HALF, HALF)
        rows = pl.ds(start, HALF)
        slot = k.slot(i)

        def add(part, values):
            where = (pl.ds(slot, 1), slice((part - 2) * D, (part - 1) * D))
            gmod[where] = gmod[where] + jnp.sum(values, axis=0, keepdims=True)

        grown = branch[rows, :]
        middle = x[rows, :].astype(f32) + k.share(slot, 2) * grown
        normal, rate = normalise(middle)
        inner = (normal * (1.0 + k.share(slot, 4)) + k.share(slot, 3)).astype(bf16)
        k.inner_s[rows, :] = inner
        live = (row_iota(HALF, 1) + start) < k.live_rows
        above = jnp.where(live, grad[rows, :].astype(f32), 0.0)
        add(5, above * (down[rows, :] + k.bn()))
        grad_down = above * k.share(slot, 5)
        gbn[...] = gbn[...] + jnp.sum(grad_down, axis=0, keepdims=True)
        down_low = grad_down.astype(bf16)
        k.down_s[rows, :] = down_low
        up = mm(inner, wu[...]) + k.bu()
        square, tanh = gelu_parts(up)
        half = 0.5 * (1.0 + tanh)
        k.hidden_s[rows, :] = (up * half).astype(bf16)
        slope = half + 0.5 * up * (1.0 - tanh * tanh) * (
            GELU_A * (1.0 + 3.0 * GELU_B * square)
        )
        grad_up = mm_t(down_low, wn[...]) * slope
        gbu[...] = gbu[...] + jnp.sum(grad_up, axis=0, keepdims=True)
        up_low = grad_up.astype(bf16)
        k.up_s[rows, :] = up_low
        grad_inner = mm_t(up_low, wu[...])
        add(3, grad_inner)
        add(4, grad_inner * normal)
        grad_middle = above + normalise_back(
            normal, rate, grad_inner * (1.0 + k.share(slot, 4))
        )
        k.mid_grad[rows, :] = grad_middle
        add(2, grad_middle * grown)
        k.branch_low[rows, :] = (grad_middle * k.share(slot, 2)).astype(bf16)
        return carry

    lax.fori_loop(0, 2, tile, 0)
    k.push("mid_grad")
    k.push("branch_low")

    def weights(j, carry):
        part = pl.ds(pl.multiple_of(j * HALF, HALF), HALF)
        hidden_t = jnp.transpose(k.hidden_s[:, part].astype(f32)).astype(bf16)
        k.gwn[part, :] = mm(hidden_t, k.down_s[...])
        return carry

    lax.fori_loop(0, FF // HALF, weights, 0)
    k.push("gwn")
    inner_t = jnp.transpose(k.inner_s[...].astype(f32)).astype(bf16)

    def halves(j, carry):
        here = pl.ds(pl.multiple_of(j * HALF, HALF), HALF)
        keep = pl.ds(pl.multiple_of(j * HALF + k.section * (FF // 2), HALF), HALF)
        send = pl.ds(pl.multiple_of(j * HALF + (1 - k.section) * (FF // 2), HALF), HALF)
        k.gwu_keep[:, here] = mm(inner_t, k.up_s[:, keep])
        k.gwu_send[:, here] = mm(inner_t, k.up_s[:, send]).astype(bf16)
        return carry

    lax.fori_loop(0, FF // 2 // HALF, halves, 0)
    k.push("gwu_keep")
    k.push("gwu_send")
    gated = k.gated()
    k.gwo[...] = mm(jnp.transpose(gated[...].astype(f32)).astype(bf16), k.branch_low[...])

    short = jnp.concatenate([gbn[...], jnp.zeros((1, FF - D), f32)], axis=1)
    k.sums[...] = jnp.concatenate(
        [gmod[0:SLOTS, :], gbu[...], short, jnp.zeros((4, FF), f32)], axis=0
    )


def mixer_backward_body(k):
    flip = k.layer == 1
    wide = k.wide
    mixed_s, low, dv_s, rows_s, cols_s = k.mixed_s, k.low, k.dv_s, k.rows_s, k.cols_s
    fill_bias(k.bias, wide)
    branch_low, wo = k.branch_low(), k.wo()

    def first(i, carry):
        start = pl.multiple_of(i * HALF, HALF)
        rows = pl.ds(start, HALF)
        if flip:
            part = mm(order_matrix(start, HALF, wide, True), branch_low[...]).astype(bf16)
        else:
            part = branch_low[rows, :]
        mixed_s[rows, :] = mm_t(part, wo[...])
        return carry

    lax.fori_loop(0, 2, first, 0)
    rows_s[...] = jnp.zeros(rows_s.shape, f32)
    cols_s[...] = jnp.zeros(cols_s.shape, f32)
    qkvg, vc, cum, cumt, o = k.qkvg(), k.vc(), k.cum(), k.cumt(), k.o()
    k.small()

    def pair(p, carry):
        lanes = lane_iota(1, PAIR)
        total = o[:, columns(p)]
        gate = qkvg[:, columns(p, 3 * D)]
        above = mixed_s[:, columns(p)]
        rate = lax.rsqrt(head_norm(total, lanes) + 1.0)
        sig = sigmoid(gate)
        grad_gate = above * (total * rate) * (sig * (1.0 + gate * (1.0 - sig)))
        low[:, columns(p, 3 * D)] = grad_gate.astype(bf16)
        grad_normed = above * (gate * sig)
        product = grad_normed * total
        inside = jnp.where(
            lanes < HEAD_DIM,
            jnp.sum(jnp.where(lanes < HEAD_DIM, product, 0.0), axis=1, keepdims=True),
            jnp.sum(jnp.where(lanes < HEAD_DIM, 0.0, product), axis=1, keepdims=True),
        ) * (1.0 / HEAD_DIM)
        grad_o = rate * grad_normed - total * (rate * rate * rate) * inside

        queries = qkvg[:, columns(p)] * SCALE
        keys = qkvg[:, columns(p, D)]
        values = vc[:, columns(p)]
        query_cat = cat_left(queries)
        grad_cat = cat_left(grad_o)
        key_high, key_low = split(keys)
        key_pair = jnp.concatenate([key_high, key_low], axis=1)
        query_t = jnp.transpose(queries)
        grad_t = jnp.transpose(grad_o)
        grad_q = []
        grad_k = []
        grad_v = []
        for e in range(2):
            mine = (lanes // HEAD_DIM) == e
            head = 2 * p + e
            key_cat = cat_right(jnp.where(mine, keys, 0.0))
            value_cat = cat_right(jnp.where(mine, values, 0.0))
            first, second = decay_factors(cum, cumt, k.bias, head)
            raw_first = mm_t(query_cat[:HALF], key_cat[:HALF])
            raw_second = mm_t(query_cat[HALF:], key_cat)
            grad_first = first * mm_t(grad_cat[:HALF], value_cat[:HALF])
            grad_second = second * mm_t(grad_cat[HALF:], value_cat)
            score_first = raw_first * first
            score_second = raw_second * second
            pull_first = grad_first * raw_first
            pull_second = grad_second * raw_second
            here = lanes == head
            rows_s[:HALF, :] = rows_s[:HALF, :] + jnp.where(
                here, jnp.sum(pull_first, axis=1, keepdims=True), 0.0
            )
            rows_s[HALF:, :] = rows_s[HALF:, :] + jnp.where(
                here, jnp.sum(pull_second, axis=1, keepdims=True), 0.0
            )
            low_cols = jnp.sum(pull_second, axis=0, keepdims=True)
            cols_s[pl.ds(head, 1), :HALF] = low_cols[:, :HALF] + jnp.sum(
                pull_first, axis=0, keepdims=True
            )
            cols_s[pl.ds(head, 1), HALF:] = low_cols[:, HALF:]
            grad_q.append(
                jnp.concatenate(
                    [
                        mm_near(grad_first, key_pair[:HALF], key_high[:HALF]),
                        mm_near(grad_second, key_pair, key_high),
                    ],
                    axis=0,
                )
            )

            def turned(source_t, block_first, block_second):
                high, low = split(source_t[e * HEAD_DIM : (e + 1) * HEAD_DIM, :])
                both = jnp.concatenate([high, low], axis=0)
                first_high, first_low = split(block_first)
                second_high, second_low = split(block_second)
                one = mm(both[:, :HALF], first_high)
                one = one[:HEAD_DIM] + one[HEAD_DIM:] + mm(high[:, :HALF], first_low)
                two = mm(both[:, HALF:], second_high)
                two = two[:HEAD_DIM] + two[HEAD_DIM:] + mm(high[:, HALF:], second_low)
                return jnp.concatenate([two[:, :HALF] + one, two[:, HALF:]], axis=1)

            grad_k.append(turned(query_t, grad_first, grad_second))
            grad_v.append(turned(grad_t, score_first, score_second))
        query_grad = jnp.where(lanes < HEAD_DIM, grad_q[0], grad_q[1]) * SCALE
        low[:, columns(p)] = query_grad.astype(bf16)
        low[:, columns(p, D)] = jnp.transpose(jnp.concatenate(grad_k, axis=0)).astype(bf16)
        dv_s[:ROWS, columns(p)] = jnp.transpose(jnp.concatenate(grad_v, axis=0))
        return carry

    lax.fori_loop(0, PAIRS, pair, 0)

    pulled = rows_s[...] - jnp.transpose(cols_s[...])
    high, middle, rest = split_three(pulled)
    upper_first = jnp.concatenate(
        [
            jnp.where(row_iota(HALF, HALF) <= lane_iota(HALF, HALF), 1.0, 0.0),
            jnp.full((HALF, HALF), 0.0, f32) + jnp.where(wide, 1.0, 0.0),
        ],
        axis=1,
    ).astype(bf16)
    upper_second = upper_first[:, :HALF]
    later = jnp.concatenate(
        [
            mm(upper_first, high) + mm(upper_first, middle) + mm(upper_first, rest),
            mm(upper_second, high[HALF:]) + mm(upper_second, middle[HALF:])
            + mm(upper_second, rest[HALF:]),
        ],
        axis=0,
    )
    grad_dp = later * (1.0 / 16.0) * sigmoid(-(k.dp()[...] + k.bd()))
    grad_bd = jnp.sum(grad_dp, axis=0, keepdims=True)
    low[:, QKVG:] = grad_dp.astype(bf16)

    dv_s[ROWS:, :] = jnp.zeros((8, D), f32)
    position = row_iota(ROWS, 1) & jnp.where(wide, ROWS - 1, HALF - 1)
    last = jnp.where(wide, ROWS - 1, HALF - 1)
    here = dv_s[0:ROWS, :]
    one = jnp.where(position <= last - 1, dv_s[1 : 1 + ROWS, :], 0.0)
    two = jnp.where(position <= last - 2, dv_s[2 : 2 + ROWS, :], 0.0)
    value = qkvg[:, 2 * D : 3 * D]
    low[:, 2 * D : 3 * D] = (k.ck(0) * here + k.ck(1) * one + k.ck(2) * two).astype(bf16)
    k.push("low")

    taps = [jnp.sum(rows * value, axis=0, keepdims=True) for rows in (here, one, two)]
    rest = jnp.concatenate([grad_bd, jnp.zeros((1, D - LANES), f32)], axis=1)
    k.sums[...] = jnp.concatenate([*taps, rest, jnp.zeros((4, D), f32)], axis=0)

    ordered_t = jnp.transpose(k.ordered()[...].astype(f32)).astype(bf16)
    gwo = k.gwo()
    gw = k.gw

    def weights(j, carry):
        part = pl.ds(pl.multiple_of(j * HALF, HALF), HALF)
        gw[:, part] = mm(ordered_t, low[:, part])
        return carry

    lax.fori_loop(0, QKVG // HALF, weights, 0)
    gw[:, QKVG : QKVG + D] = gwo[...]
    gw[:, QKVG + D :] = mm(ordered_t, low[:, QKVG:])

    def halves(j, carry):
        here = pl.ds(pl.multiple_of(j * HALF, HALF), HALF)
        keep = pl.ds(pl.multiple_of(j * HALF + k.section * GROUP, HALF), HALF)
        send = pl.ds(pl.multiple_of(j * HALF + (1 - k.section) * GROUP, HALF), HALF)
        k.gw_keep[:, here] = gw[:, keep]
        k.gw_send[:, here] = gw[:, send].astype(bf16)
        return carry

    lax.fori_loop(0, GROUP // HALF, halves, 0)


def input_backward_body(k):
    flip = k.layer == 1
    wide = k.wide
    gmod, mixed_s, perm_s = k.gmod, k.mixed_s, k.perm_s
    gmod[...] = jnp.zeros(gmod.shape, f32)
    low, w_qk, w_vgd = k.low(), k.w_qk(), k.w_vgd()

    def inner_grad(i, carry):
        rows = pl.ds(pl.multiple_of(i * HALF, HALF), HALF)
        mixed_s[rows, :] = mm_t(low[rows, : 2 * D], w_qk[...]) + mm_t(
            low[rows, 2 * D :], w_vgd[...]
        )
        return carry

    lax.fori_loop(0, 2, inner_grad, 0)
    if flip:
        high, middle, rest = split_three(mixed_s[...])
        perm_s[:, :D] = high
        perm_s[:, D : 2 * D] = middle
        perm_s[:, 2 * D :] = rest
    x, mid_grad = k.x(), k.mid_grad()
    k.mods()

    def tile(i, carry):
        start = pl.multiple_of(i * HALF, HALF)
        rows = pl.ds(start, HALF)
        slot = k.slot(i)
        if flip:
            three = mm(order_matrix(start, HALF, wide, False), perm_s[...])
            grad = three[:, :D] + three[:, D : 2 * D] + three[:, 2 * D :]
        else:
            grad = mixed_s[rows, :]
        normal, rate = normalise(x[rows, :].astype(f32))
        where = (pl.ds(slot, 1), slice(0, D))
        gmod[where] = gmod[where] + jnp.sum(grad, axis=0, keepdims=True)
        where = (pl.ds(slot, 1), slice(D, 2 * D))
        gmod[where] = gmod[where] + jnp.sum(grad * normal, axis=0, keepdims=True)
        total = mid_grad[rows, :] + normalise_back(normal, rate, grad * (1.0 + k.share(slot, 1)))
        k.gx[rows, :] = total
        k.gx_low[rows, :] = total.astype(bf16)
        return carry

    lax.fori_loop(0, 2, tile, 0)
    k.push("gx_low")
    k.push("gx")
    ffn, mixer = k.ffn_sums(), k.mixer_sums()
    k.mod_low[...] = jnp.concatenate([gmod[...], ffn[...]], axis=1).astype(bf16)
    half = 2 * D
    rest = ffn[0:1, :] + ffn[1:2, :]
    k.sums[...] = jnp.concatenate(
        [
            gmod[0:1, :] + gmod[1:2, :],
            rest[:, :half],
            rest[:, half:],
            ffn[2:3, :half],
            ffn[2:3, half:],
            jnp.concatenate([ffn[3:4, :D], mixer[0:1, :]], axis=1),
            jnp.concatenate([mixer[1:2, :], mixer[2:3, :]], axis=1),
            jnp.concatenate([mixer[3:4, :], jnp.zeros((1, D), f32)], axis=1),
        ],
        axis=0,
    )


ANY = pl.BlockSpec(memory_space=pl.ANY)
VMEM = pl.BlockSpec(memory_space=pltpu.VMEM)
HBM = pl.BlockSpec(memory_space=pltpu.HBM)


def call(body, layer, layouts, ins, outs, scratch, flops):
    arrays = []
    counts = []
    kept = []
    places = []
    for kind, given, part in ins.values():
        places.extend([ANY] * 2 if kind == "own" else [HBM])
        given = given if kind == "own" else (given,)
        arrays.extend(given)
        counts.append(len(given))
        rows, wide = given[0].shape[-2:]
        start, stop = part or (0, wide)
        kept.append(pltpu.VMEM((rows, stop - start), given[0].dtype))

    def kernel(*refs):
        refs = list(refs)
        take = lambda count: [refs.pop(0) for _ in range(count)]
        (layouts_ref,) = take(1)
        sources = [take(count) for count in counts]
        targets = take(len(outs))
        buffers = take(len(ins))
        results = take(len(outs))
        rest = take(len(scratch))
        in_sems, out_sems = refs
        k = Kernel(layer, layouts_ref)
        for number, (name, (kind, _, part)) in enumerate(ins.items()):
            given = sources[number]
            if part is not None:
                given = [ref.at[:, part[0] : part[1]] for ref in given]
            setattr(k, name, k.load(kind, given, buffers[number], in_sems.at[number]))
        k.results = {}
        for number, name in enumerate(outs):
            setattr(k, name, results[number])
            k.results[name] = (results[number], targets[number], out_sems.at[number])
        for name, ref in zip(scratch, rest):
            setattr(k, name, ref)
        body(k)
        k.finish()

    return pl.pallas_call(
        kernel,
        out_shape=[jax.ShapeDtypeStruct(shape, kind) for shape, kind, _ in outs.values()],
        in_specs=[pl.BlockSpec(memory_space=pltpu.SMEM)] + places,
        out_specs=[HBM if for_kernel else ANY for _, _, for_kernel in outs.values()],
        scratch_shapes=kept
        + [pltpu.VMEM(shape, kind) for shape, kind, _ in outs.values()]
        + [pltpu.VMEM(shape, kind) for shape, kind in scratch.values()]
        + [pltpu.SemaphoreType.DMA((len(ins),)), pltpu.SemaphoreType.DMA((len(outs),))],
        compiler_params=pltpu.CompilerParams(vmem_limit_bytes=56 * 1024 * 1024),
        cost_estimate=pl.CostEstimate(flops=flops, bytes_accessed=4 << 20, transcendentals=0),
    )(layouts, *arrays)


def own(pair, part=None):
    return ("own", pair, part)


def plain(array):
    return ("plain", array, None)


def micro(array):
    return ("micro", array, None)


AT_UP = (0, FF)
AT_QK = (FF, FF + 2 * D)
AT_OUT = (FF + 2 * D, FF + 3 * D)


def attn_forward(layer, layouts, x, mods, small, packed, vgd):
    return call(
        attn_forward_body,
        layer,
        layouts,
        dict(
            x=micro(x),
            mods=own(mods),
            w_qk=own(packed, AT_QK),
            w_vgd=own(vgd),
            small=own(small),
        ),
        dict(
            ordered=((ROWS, D), bf16, True),
            qkvg=((ROWS, QKVG), f32, True),
            dp=((ROWS, LANES), f32, True),
            vc=((ROWS, D), f32, True),
            cum=((ROWS, LANES), f32, True),
            cumt=((LANES, ROWS), f32, True),
            o=((ROWS, D), f32, True),
            gated=((ROWS, D), bf16, True),
        ),
        dict(
            inner=((ROWS, D), bf16),
            vpad=((ROWS + 8, D), f32),
            bias=((HALF, ROWS), f32),
        ),
        8 * 10**9,
    )


def ffn_forward(layer, layouts, x, mods, small, gated, packed, down):
    return call(
        ffn_forward_body,
        layer,
        layouts,
        dict(
            gated=plain(gated),
            x=micro(x),
            wo=own(packed, AT_OUT),
            mods=own(mods),
            small=own(small),
            wu=own(packed, AT_UP),
            wn=own(down),
        ),
        dict(
            out=((ROWS, D), bf16, True),
            branch=((ROWS, D), f32, True),
            down=((ROWS, D), f32, True),
        ),
        {},
        5 * 10**9,
    )


def ffn_backward(layer, layouts, x, mods, small, gated, branch, down_raw, grad, packed, down):
    return call(
        ffn_backward_body,
        layer,
        layouts,
        dict(
            mods=own(mods),
            small=own(small),
            x=micro(x),
            grad=micro(grad),
            branch=plain(branch),
            down=plain(down_raw),
            wu=own(packed, AT_UP),
            wn=own(down),
            gated=plain(gated),
        ),
        dict(
            mid_grad=((ROWS, D), f32, True),
            branch_low=((ROWS, D), bf16, True),
            gwo=((D, D), f32, True),
            gwu_keep=((D, FF // 2), f32, False),
            gwu_send=((D, FF // 2), bf16, False),
            gwn=((FF, D), f32, False),
            sums=((8, FF), f32, True),
        ),
        dict(
            hidden_s=((ROWS, FF), bf16),
            inner_s=((ROWS, D), bf16),
            up_s=((ROWS, FF), bf16),
            down_s=((ROWS, D), bf16),
            gmod=((8, FF), f32),
            gbu=((1, FF), f32),
            gbn=((1, D), f32),
        ),
        12 * 10**9,
    )


def mixer_backward(layer, layouts, small, saved, branch_low, gwo, packed):
    ordered, qkvg, dp, vc, cum, cumt, o = saved
    return call(
        mixer_backward_body,
        layer,
        layouts,
        dict(
            branch_low=plain(branch_low),
            wo=own(packed, AT_OUT),
            qkvg=plain(qkvg),
            vc=plain(vc),
            cum=plain(cum),
            cumt=plain(cumt),
            o=plain(o),
            small=own(small),
            dp=plain(dp),
            ordered=plain(ordered),
            gwo=plain(gwo),
        ),
        dict(
            low=((ROWS, QKVG + LANES), bf16, True),
            gw_keep=((D, GROUP), f32, False),
            gw_send=((D, GROUP), bf16, False),
            sums=((8, D), f32, True),
        ),
        dict(
            mixed_s=((ROWS, D), f32),
            dv_s=((ROWS + 8, D), f32),
            rows_s=((ROWS, LANES), f32),
            cols_s=((LANES, ROWS), f32),
            bias=((HALF, ROWS), f32),
            gw=((D, 2 * GROUP), f32),
        ),
        15 * 10**9,
    )


def input_backward(layer, layouts, x, mods, low, mid_grad, ffn_sums, mixer_sums, packed, vgd):
    return call(
        input_backward_body,
        layer,
        layouts,
        dict(
            low=plain(low),
            w_qk=own(packed, AT_QK),
            w_vgd=own(vgd),
            x=micro(x),
            mid_grad=plain(mid_grad),
            mods=own(mods),
            ffn_sums=plain(ffn_sums),
            mixer_sums=plain(mixer_sums),
        ),
        dict(
            gx=((ROWS, D), f32, False),
            gx_low=((ROWS, D), bf16, True),
            mod_low=((8, 6 * D), bf16, False),
            sums=((8, 2 * D), f32, False),
        ),
        dict(
            mixed_s=((ROWS, D), f32),
            perm_s=((ROWS, 3 * D), bf16),
            gmod=((8, 2 * D), f32),
        ),
        4 * 10**9,
    )


def small_kernel(b_up, b_down, taps, b_decay, packed):
    packed[...] = jnp.zeros(packed.shape, f32)
    packed[0:1, :] = b_up[...]
    packed[1:2, :D] = b_down[...]
    packed[2:5, :D] = taps[0]
    packed[5:6, :HEADS] = b_decay[...]


def pack_small(b_up, b_down, taps, b_decay):
    return pl.pallas_call(
        small_kernel,
        out_shape=jax.ShapeDtypeStruct((8, FF), f32),
        in_specs=[VMEM] * 4,
        out_specs=VMEM,
    )(b_up, b_down, taps, b_decay)


def pack_kernel(*refs):
    packed = refs[-1]
    at = 0
    for ref in refs[:-1]:
        width = ref.shape[1]
        if width % LANES:
            packed[:, at:] = jnp.zeros((packed.shape[0], packed.shape[1] - at), packed.dtype)
        packed[:, at : at + width] = ref[...]
        at += width


def pack(*arrays):
    total = sum(-(-array.shape[1] // LANES) * LANES for array in arrays)
    return pl.pallas_call(
        pack_kernel,
        out_shape=jax.ShapeDtypeStruct((arrays[0].shape[0], total), arrays[0].dtype),
        in_specs=[VMEM] * len(arrays),
        out_specs=VMEM,
    )(*arrays)


def swap(values):
    return lax.ppermute(values, "section", [(0, 1), (1, 0)])


def row_bits():
    bits = lax.axis_size("row").bit_length() - 1
    third = bits // 3
    return (
        tuple(range(third)),
        tuple(range(third, 2 * third)),
        tuple(range(2 * third, bits)),
    )


def partner(values, bit):
    size = lax.axis_size("row")
    return lax.ppermute(values, "row", [(i, i ^ (1 << bit)) for i in range(size)])


def axis_of(bit):
    return lax.axis_size("row").bit_length() - 2 - bit


def bit_of(bit):
    return (lax.axis_index("row") >> bit) & 1


def single(values):
    return values.reshape((1,) * (lax.axis_size("row").bit_length() - 1) + values.shape)


def join(held, other, bit):
    return jnp.where(
        bit_of(bit) == 0,
        jnp.concatenate([held, other], axis=axis_of(bit)),
        jnp.concatenate([other, held], axis=axis_of(bit)),
    )


def flat(held):
    return held.reshape(-1, held.shape[-1])


def by_bits(values):
    bits = lax.axis_size("row").bit_length() - 1
    return values.reshape((2,) * bits + values.shape[1:])


def cut(held, bit):
    axis = axis_of(bit)
    mine = bit_of(bit)
    sent = lax.dynamic_index_in_dim(held, 1 - mine, axis, keepdims=True)
    kept = lax.dynamic_index_in_dim(held, mine, axis, keepdims=True)
    return sent, kept


def lock(*arrays):
    return lax.optimization_barrier(arrays)


class Scatter:
    def __init__(self, values):
        self.held = by_bits(values)
        self.kept = None

    def ready(self, bit):
        sent, self.kept = cut(self.held, bit)
        return sent.astype(bf16)

    def take(self, other):
        self.held = self.kept + other.astype(f32)

    def result(self):
        return self.held.reshape(self.held.shape[-2:])


class Gather:
    def __init__(self, values):
        self.held = single(values)

    def ready(self, bit):
        self.bit = bit
        return self.held

    def take(self, other):
        self.held = join(self.held, other, self.bit)


class Total:
    def __init__(self, values):
        self.held = values

    def ready(self, bit):
        return self.held

    def take(self, other):
        self.held = self.held + other


def begin(chains, bit):
    return [chain.ready(bit) for chain in chains]


def send(arrays, bit):
    return [partner(array, bit) for array in arrays]


def end(chains, arrays):
    for chain, array in zip(chains, arrays):
        chain.take(array)


def on_device(
    tokens, conditions, output_grad, layouts,
    w_ada, b_ada, w_query, w_key, w_value, w_gate, w_out, w_decay, b_decay, conv_kernel,
    w_up, b_up, w_down, b_down,
):
    section = lax.axis_index("section")
    devices = lax.axis_size("row")
    is_first = section == 0
    shard = w_query.shape[1]
    along_x, along_y, along_z = row_bits()
    plane = along_x + along_y
    every = plane + along_z

    def pick(pair):
        return jnp.where(is_first, pair[0], pair[1])

    def pick_other(pair):
        return jnp.where(is_first, pair[1], pair[0])

    def both(values):
        return values, swap(values)

    def groups(run):
        rest = [bit for bit in every if bit not in run]
        numbers = lambda bits: [
            sum(((i >> place) & 1) << bit for place, bit in enumerate(bits))
            for i in range(1 << len(bits))
        ]
        return [[base + step for step in numbers(run)] for base in numbers(rest)]

    ada = lax.all_gather(w_ada[0], "row", axis_index_groups=groups(along_z), tiled=True)
    ada = lax.all_gather(ada, "row", axis_index_groups=groups(plane), tiled=True)
    height, width = 1 << len(along_z), 1 << len(plane)

    group_a = [Gather(pack(w_up[0], w_query[0], w_key[0], w_out[0]))]
    group_b = [Gather(pack(w_value[0], w_gate[0], w_decay[0])), Gather(w_down[0])]
    chains = group_a + group_b
    for bit in reversed(along_z):
        end(chains, lock(*send(begin(chains, bit), bit)))
    for bit_a, bit_b in zip(plane, along_y + along_x):
        others_a = send(begin(group_a, bit_a), bit_a)
        others_b = send(begin(group_b, bit_b), bit_b)
        others = lock(*others_a, *others_b)
        end(chains, others)
    packed, vgd, down = [both(flat(chain.held)) for chain in chains]

    lifted_own = jax.nn.silu(conditions.astype(f32)).astype(bf16).reshape(MICRO * SLOTS, D)
    lifted_cut = lifted_own.reshape(MICRO * SLOTS, height, width, shard).swapaxes(1, 2)
    mods = both(mm(lifted_cut.reshape(MICRO * SLOTS, D), ada) + b_ada[0])
    smalls = both(pack_small(b_up, b_down, conv_kernel, b_decay))

    late, _ = lock(lifted_own, mods[0])
    lifted_rows = Gather(late)
    for bit in reversed(every):
        end([lifted_rows], send(begin([lifted_rows], bit), bit))
    lifted_rows = lax.dynamic_slice_in_dim(
        flat(lifted_rows.held), lax.axis_index("row") * shard, shard, 1
    )

    x = tokens
    kept = []
    acts = []
    for l in range(2):
        *saved, gated = attn_forward(l, layouts, x, mods, smalls, packed, vgd)
        out, branch, down_raw = ffn_forward(l, layouts, x, mods, smalls, gated, packed, down)
        kept.append((x, saved, gated, branch, down_raw))
        acts.append(out)
        x = out[None]

    def ffn_step(l, grad):
        x, saved, gated, branch, down_raw = kept[l]
        mid_grad, branch_low, gwo, keep, sent, gwn, sums = ffn_backward(
            l, layouts, x, mods, smalls, gated, branch, down_raw, grad, packed, down
        )
        pair = gwn.reshape(devices, 2, FF // devices // 2, D)
        down_keep = lax.dynamic_index_in_dim(pair, section, 1, keepdims=False)
        down_send = lax.dynamic_index_in_dim(pair, 1 - section, 1, keepdims=False).astype(bf16)
        return (branch_low, gwo), mid_grad, (sent, down_send), (keep, down_keep), sums

    def mixer_step(l, carried):
        return mixer_backward(l, layouts, smalls, kept[l][1], *carried, packed)

    def input_step(l, low, mid_grad, ffn_sums, mixer_sums):
        return input_backward(
            l, layouts, kept[l][0], mods, low, mid_grad, ffn_sums, mixer_sums, packed, vgd
        )

    def ffn_chains(keep, others):
        up_half = keep[0] + others[0].astype(f32)
        down_half = keep[1] + others[1].astype(f32)
        return [Scatter(up_half.reshape(devices, shard, FF // 2)), Scatter(down_half)]

    def attn_chain(keep, other):
        return [Scatter((keep + other.astype(f32)).reshape(devices, shard, GROUP))]

    def steps(chains, bits):
        for bit in bits[:-1]:
            end(chains, send(begin(chains, bit), bit))
        return begin(chains, bits[-1])

    def divide(arrays, *counts):
        parts = []
        for count in counts:
            parts.append(list(arrays[:count]))
            arrays = arrays[count:]
        return parts

    x_bits, y_bits, z_bits = along_x, along_y, along_z
    carried, mid_grad, f2_send, f2_keep, f2_sums = ffn_step(1, output_grad)
    acts_send = pick_other(acts)
    *carried, acts_send, s0, s1 = lock(*carried, acts_send, *f2_send)
    f2_other = [swap(s0), swap(s1)]
    acts_other = swap(acts_send)
    low, a2_keep, a2_send, m2_sums = mixer_step(1, carried)
    low, acts_other, *f2_other = lock(low, acts_other, *f2_other)
    f2 = ffn_chains(f2_keep, f2_other)
    f2_sent = steps(f2, x_bits)
    low, a2_send, *f2_sent = lock(low, a2_send, *f2_sent)
    f2_other = send(f2_sent, x_bits[-1])
    a2_other = swap(a2_send)
    gx_two, grad, mod_low_two, sums_two = input_step(1, low, mid_grad, f2_sums, m2_sums)
    grad, a2_other, mod_low_two = lock(grad, a2_other, mod_low_two[:SLOTS])
    a2 = attn_chain(a2_keep, a2_other)
    mod2 = [Gather(mod_low_two)]
    a2_sent = steps(a2 + mod2, x_bits)
    grad, *a2_sent = lock(grad, *a2_sent)
    a2_other = send(a2_sent, x_bits[-1])

    carried, mid_grad, f1_send, f1_keep, f1_sums = ffn_step(0, grad[None])
    locked = lock(*carried, *f1_send, *f2_other, *a2_other)
    carried, f1_send, locked = divide(locked, 2, 2, 4)
    f1_other = lock(*[swap(array) for array in f1_send])
    two = f2 + a2 + mod2
    end(two, locked)
    two_sent = steps(two, y_bits)
    f1 = ffn_chains(f1_keep, f1_other)
    f1_sent = steps(f1, x_bits)
    carried, two_sent, f1_sent = divide(lock(*carried, *two_sent, *f1_sent), 2, 4, 2)
    two_other = send(two_sent, y_bits[-1])
    f1_other = send(f1_sent, x_bits[-1])
    low, a1_keep, a1_send, m1_sums = mixer_step(0, carried)
    low, *locked = lock(low, *two_other, *f1_other)
    end(two + f1, locked)
    two_sent = steps(two, z_bits)
    f1_sent = steps(f1, y_bits)
    low, a1_send, *locked = lock(low, a1_send, *two_sent, *f1_sent)
    two_sent, f1_sent = divide(locked, 4, 2)
    a1_other = swap(a1_send)
    two_other = send(two_sent, z_bits[-1])
    f1_other = send(f1_sent, y_bits[-1])
    gx_one, _, mod_low_one, sums_one = input_step(0, low, mid_grad, f1_sums, m1_sums)
    gx_send = pick_other((gx_one, gx_two))
    mod_low_one = mod_low_one[:SLOTS]
    a1_other, mod_low_one, sums_one, gx_send, *locked = lock(
        a1_other, mod_low_one, sums_one, gx_send, *two_other, *f1_other
    )
    end(two + f1, locked)
    mod1 = [Gather(mod_low_one)]
    totals = [Total(jnp.concatenate([sums_one, sums_two], axis=0))]
    one = attn_chain(a1_keep, a1_other) + mod1 + totals
    gx_other = swap(gx_send)
    mod_other = swap(pick_other((mod_low_one, mod_low_two)))
    for bit in plane:
        end(one, lock(*send(begin(one, bit), bit)))
    one = one + f1
    for bit in z_bits:
        end(one, lock(*send(begin(one, bit), bit)))

    lifted_mine = lax.dynamic_index_in_dim(
        lifted_rows.reshape(devices, MICRO, SLOTS, shard), section, 1, keepdims=False
    ).reshape(devices * SLOTS, shard)

    def summed(ffn, attn, mod, total):
        ada_term = lax.dot_general(
            lifted_mine, flat(mod.held), (((0,), (0,)), ((), ())), preferred_element_type=f32
        )
        return [attn.result(), ffn[0].result(), ffn[1].result(), ada_term, total]

    total = totals[0].held
    sums = (
        summed(f1, one[0], mod1[0], total[:8]),
        summed(f2, a2[0], mod2[0], total[8:]),
    )
    mine = [pick(pair) for pair in zip(*sums)]
    other = [swap(pick_other(pair)) for pair in zip(*sums)]

    def halves(number, axis):
        mine_half, other_half = mine[number], other[number]
        return jnp.concatenate(
            [pick((mine_half, other_half)), pick_other((mine_half, other_half))], axis=axis
        )

    attn_total = halves(0, 1)
    up_total = halves(1, 1)
    down_total = halves(2, 0)
    grad_w_ada = mine[3] + other[3]
    small = mine[4] + other[4]

    mod_own = pick((mod_low_one, mod_low_two))
    mod_both = jnp.concatenate([pick((mod_own, mod_other)), pick_other((mod_own, mod_other))])
    grad_lifted = mm_t(mod_both, ada)
    grad_lifted = (grad_lifted + swap(grad_lifted)).reshape(MICRO * SLOTS, width, height, shard)
    grad_lifted = grad_lifted.swapaxes(1, 2).reshape(MICRO, SLOTS, D)
    _, pull_silu = jax.vjp(jax.nn.silu, conditions.astype(f32))
    (cond_grads,) = pull_silu(grad_lifted)

    def assembled(pair, other):
        mine = pick(pair)
        return jnp.stack([pick((mine, other)), pick_other((mine, other))])

    return (
        assembled(acts, acts_other)[None],
        assembled((gx_one, gx_two), gx_other)[None],
        cond_grads,
        grad_w_ada[None],
        small[0:3].reshape(1, 6 * D),
        attn_total[None, :, :D],
        attn_total[None, :, D : 2 * D],
        attn_total[None, :, 2 * D : 3 * D],
        attn_total[None, :, 3 * D : 4 * D],
        attn_total[None, :, 4 * D : 5 * D],
        attn_total[None, :, 5 * D : 5 * D + HEADS],
        small[7:8, :HEADS],
        jnp.concatenate([small[5, D:], small[6]]).reshape(1, 3, D),
        up_total[None],
        small[3:5].reshape(1, FF),
        down_total[None],
        small[5:6, :D],
    )


def solution(mesh):
    rows = P(None, "row", None)
    mats = P("section", "row", None)
    vector = P("section", None)
    in_specs = (
        rows, rows, rows, P(None, "row"),
        mats, vector, mats, mats, mats, mats, mats, mats, vector, P("section", None, None),
        mats, vector, mats, vector,
    )
    blocks = P("section", None, "row", None)
    out_specs = (
        blocks, blocks, rows,
        mats, vector, mats, mats, mats, mats, mats, mats, vector, P("section", None, None),
        mats, vector, mats, vector,
    )
    return jax.shard_map(
        on_device, mesh=mesh, in_specs=in_specs, out_specs=out_specs, check_vma=False
    )
```

profile of v0, /device:TPU:0, one launch (start us, length us, event | category | flops | bytes accessed | tf_op | source)
XLA Modules:
  0.0 349.5 jit_solution(17281127133499136368)
XLA Ops:
  8.8 4.0 %collective-permute-start.1 = (bf16[1,1,1,1,24,2688]{5,4,3,2,1,0:T(8,128)(2,1)}, bf16[1,1,1,1,24,2688]{5,4,3,2,1,0:T(8,128)(2,1)S(1)}, u32[]{:S(2)}, u32[]{:S(2)}) collective-permute-start(bf16[1,1,1,1,24,2688]{5,4,3,2,1,0:T(8,128)(2,1)} %bitcast.192), channel_id=1, source_target_pairs={{0,8},{1,9},{2,10},{3,11},{4,12},{5,13},{6,14},{7,15},{8,0},{9,1},... | collective-permute-start | bytes 387080 | tf_op jit(solution)/shard_map/ppermute | solution.py:952
  15.6 2.9 collective-permute-start.3
  18.5 17.8 %all-gather = bf16[1,96,2304]{2,1,0:T(8,128)(2,1)} all-gather(bf16[1,24,2304]{2,1,0:T(8,128)(2,1)} %param.22), channel_id=2, replica_groups={{0,4,8,12},{1,5,9,13},{2,6,10,14},{3,7,11,15},{16,20,24,28},{17,21,25,2..., dimensions={1}, use_global_device_ids=true | all-gather | bytes 552960 | tf_op jit(solution)/shard_map/all_gather | solution.py:1078
  38.7 1.9 collective-permute-start.5
  41.0 5.7 %collective-permute-done.5 = bf16[2,1,1,1,24,896]{5,4,0,1,3,2:T(8,128)(2,1)S(1)} collective-permute-done((bf16[2,1,1,1,24,896]{5,4,0,1,3,2:T(8,128)(2,1)S(1)}, bf16[2,1,1,1,24,896]{5,4,0,1,3,2:T(8,128)(2,1)S(1)}, u32[]{:S(2)}, u32[]{:S(2)}) %collective-permute-start.5) | collective-permute-done | bytes 86048 | tf_op jit(solution)/shard_map/ppermute | solution.py:952
  52.4 5.0 %collective-permute-done.8 = bf16[2,2,1,1,24,896]{5,4,0,1,3,2:T(8,128)(2,1)S(1)} collective-permute-done((bf16[2,2,1,1,24,896]{5,4,0,1,3,2:T(8,128)(2,1)S(1)}, bf16[2,2,1,1,24,896]{5,4,0,1,3,2:T(8,128)(2,1)S(1)}, u32[]{:S(2)}, u32[]{:S(2)}) %collective-permute-start.8) | collective-permute-done | bytes 172064 | tf_op jit(solution)/shard_map/ppermute | solution.py:952
  57.5 4.0 %collective-permute-done.9 = bf16[2,2,1,1,96,384]{5,4,0,1,3,2:T(8,128)(2,1)S(1)} collective-permute-done((bf16[2,2,1,1,96,384]{5,4,0,1,3,2:T(8,128)(2,1)S(1)}, bf16[2,2,1,1,96,384]{5,4,0,1,3,2:T(8,128)(2,1)S(1)}, u32[]{:S(2)}, u32[]{:S(2)}) %collective-permute-start.9) | collective-permute-done | bytes 294944 | tf_op jit(solution)/shard_map/ppermute | solution.py:952
  66.6 25.8 %collective-permute-done.11 = bf16[2,2,2,1,24,896]{5,4,0,1,3,2:T(8,128)(2,1)S(1)} collective-permute-done((bf16[2,2,2,1,24,896]{5,4,0,1,3,2:T(8,128)(2,1)S(1)}, bf16[2,2,2,1,24,896]{5,4,0,1,3,2:T(8,128)(2,1)S(1)}, u32[]{:S(2)}, u32[]{:S(2)}) %collective-permute-start.11) | collective-permute-done | bytes 344096 | tf_op jit(solution)/shard_map/ppermute | solution.py:952
  92.4 2.1 collective-permute-done.10
  100.5 2.5 collective-permute-start.47
  106.7 2.1 collective-permute-done.48
  109.2 3.4 collective-permute-done.49
  118.7 9.3 %shard_map.308 = (bf16[512,384]{1,0:T(8,128)(2,1)}, f32[512,1536]{1,0:T(8,128)}, f32[512,128]{1,0:T(8,128)}, f32[512,384]{1,0:T(8,128)}, f32[512,128]{1,0:T(8,12...) custom-call(s32[2,1]{1,0:T(2,128)} %copy.69.refs_0_, bf16[2,512,384]{2,1,0:T(8,128)(2,1)} %refs_6_.3, ...), custom_call_target="tpu_custom_call" | custom-call | flops 8000000000 | bytes 4194304 | tf_op jit(solution)/shard_map/pallas_call | solution.py:707
  128.1 7.3 %shard_map.309 = (bf16[512,384]{1,0:T(8,128)(2,1)}, f32[512,384]{1,0:T(8,128)}, f32[512,384]{1,0:T(8,128)}) custom-call(s32[2,1]{1,0:T(2,128)} %copy.69.refs_0_, bf16[512,384]{1,0:T(8,128)(2,1)} %get-tuple-element.170.refs_1_.refs_13_, bf16[2,512,384]{2,1,0:T(8,128)(2,1)} %refs_6_.3, bf16[384,2688]{1,0:T(8,128)(2,1)} %bitcast.32.refs_4_.refs_3_.refs_9_.refs_2_, ...), custom_call_target="tpu_custom_call" | custom-call | flops 5000000000 | bytes 4194304 | tf_op jit(solution)/shard_map/pallas_call | solution.py:707
  135.4 10.3 %shard_map.310 = (bf16[512,384]{1,0:T(8,128)(2,1)}, f32[512,1536]{1,0:T(8,128)}, f32[512,128]{1,0:T(8,128)}, f32[512,384]{1,0:T(8,128)}, f32[512,128]{1,0:T(8,12...) custom-call(s32[2,1]{1,0:T(2,128)} %copy.69.refs_0_, bf16[1,512,384]{2,1,0:T(8,128)(2,1)} %bitcast.179, ...), custom_call_target="tpu_custom_call" | custom-call | flops 8000000000 | bytes 4194304 | tf_op jit(solution)/shard_map/pallas_call | solution.py:707
  145.7 7.3 %shard_map.311 = (bf16[512,384]{1,0:T(8,128)(2,1)}, f32[512,384]{1,0:T(8,128)}, f32[512,384]{1,0:T(8,128)}) custom-call(s32[2,1]{1,0:T(2,128)} %copy.69.refs_0_, bf16[512,384]{1,0:T(8,128)(2,1)} %get-tuple-element.173.refs_1_.refs_13_, bf16[1,512,384]{2,1,0:T(8,128)(2,1)} %bitcast.180, bf16[384,2688]{1,0:T(8,128)(2,1)} %bitcast.32.refs_4_.refs_3_.refs_9_.refs_2_, ...), custom_call_target="tpu_custom_call" | custom-call | flops 5000000000 | bytes 4194304 | tf_op jit(solution)/shard_map/pallas_call | solution.py:707
  153.0 13.1 %shard_map.312 = (f32[512,384]{1,0:T(8,128)}, bf16[512,384]{1,0:T(8,128)(2,1)}, f32[384,384]{1,0:T(8,128)}, f32[384,768]{1,0:T(8,128)}, bf16[384,768]{1,0:T(8,12...) custom-call(s32[2,1]{1,0:T(2,128)} %copy.69.refs_0_, f32[4,2304]{1,0:T(4,128)} %copy-done.37, f32[4,2304]{1,0:T(4,128)} %copy-done.46, ...), custom_call_target="tpu_custom_call" | custom-call | flops 12000000000 | bytes 4194304 | tf_op jit(solution)/shard_map/pallas_call | solution.py:707
  168.6 16.1 %shard_map.313 = (bf16[512,1664]{1,0:T(8,128)(2,1)}, f32[384,1024]{1,0:T(8,128)}, bf16[384,1024]{1,0:T(8,128)(2,1)}, f32[8,384]{1,0:T(8,128)}) custom-call(s32[2,1]{1,0:T(2,128)} %copy.69.refs_0_, bf16[512,384]{1,0:T(8,128)(2,1)} %get-tuple-element.181.refs_1_, bf16[384,2688]{1,0:T(8,128)(2,1)} %bitcast.32.refs_4_.refs_3_.refs_9_.refs_2_, ...), custom_call_target="tpu_custom_call" | custom-call | flops 15000000512 | bytes 4194304 | tf_op jit(solution)/shard_map/pallas_call | solution.py:707
  186.5 6.6 %shard_map.314 = (f32[512,384]{1,0:T(8,128)}, bf16[512,384]{1,0:T(8,128)(2,1)}, bf16[8,2304]{1,0:T(8,128)(2,1)}, f32[8,768]{1,0:T(8,128)}) custom-call(s32[2,1]{1,0:T(2,128)} %copy.69.refs_0_, bf16[512,1664]{1,0:T(8,128)(2,1)} %get-tuple-element.200.refs_1_, bf16[384,2688]{1,0:T(8,128)(2,1)} %bitcast.32.refs_4_.refs_3_.refs_9_.refs_2_, ...), custom_call_target="tpu_custom_call" | custom-call | flops 4000000000 | bytes 4194304 | tf_op jit(solution)/shard_map/pallas_call | solution.py:707
  198.7 13.2 %shard_map.315 = (f32[512,384]{1,0:T(8,128)}, bf16[512,384]{1,0:T(8,128)(2,1)}, f32[384,384]{1,0:T(8,128)}, f32[384,768]{1,0:T(8,128)}, bf16[384,768]{1,0:T(8,12...) custom-call(s32[2,1]{1,0:T(2,128)} %copy.69.refs_0_, f32[4,2304]{1,0:T(4,128)} %copy-done.37, f32[4,2304]{1,0:T(4,128)} %copy-done.46, ...), custom_call_target="tpu_custom_call" | custom-call | flops 12000000000 | bytes 4194304 | tf_op jit(solution)/shard_map/pallas_call | solution.py:707
  213.2 5.0 %collective-permute-done.24 = bf16[1,1,1,1,2,2304]{5,4,3,2,1,0:T(2,128)(2,1)S(1)} collective-permute-done((bf16[1,1,1,1,2,2304]{5,4,3,2,1,0:T(2,128)(2,1)S(1)}, bf16[1,1,1,1,2,2304]{5,4,3,2,1,0:T(2,128)(2,1)S(1)}, u32[]{:S(2)}, u32[]{:S(2)}) %collective-permute-start.24) | collective-permute-done | bytes 9248 | tf_op jit(solution)/shard_map/ppermute | solution.py:952
  229.0 16.0 %shard_map.316 = (bf16[512,1664]{1,0:T(8,128)(2,1)}, f32[384,1024]{1,0:T(8,128)}, bf16[384,1024]{1,0:T(8,128)(2,1)}, f32[8,384]{1,0:T(8,128)}) custom-call(s32[2,1]{1,0:T(2,128)} %copy.69.refs_0_, bf16[512,384]{1,0:T(8,128)(2,1)} %get-tuple-element.233.refs_1_, bf16[384,2688]{1,0:T(8,128)(2,1)} %bitcast.32.refs_4_.refs_3_.refs_9_.refs_2_, ...), custom_call_target="tpu_custom_call" | custom-call | flops 15000000512 | bytes 4194304 | tf_op jit(solution)/shard_map/pallas_call | solution.py:707
  250.1 2.5 collective-permute-done.34
  260.3 5.9 %shard_map.317 = (f32[512,384]{1,0:T(8,128)}, bf16[512,384]{1,0:T(8,128)(2,1)}, bf16[8,2304]{1,0:T(8,128)(2,1)}, f32[8,768]{1,0:T(8,128)}) custom-call(s32[2,1]{1,0:T(2,128)} %copy.69.refs_0_, bf16[512,1664]{1,0:T(8,128)(2,1)} %get-tuple-element.257.refs_1_, bf16[384,2688]{1,0:T(8,128)(2,1)} %bitcast.32.refs_4_.refs_3_.refs_9_.refs_2_, ...), custom_call_target="tpu_custom_call" | custom-call | flops 4000000000 | bytes 4194304 | tf_op jit(solution)/shard_map/pallas_call | solution.py:707
  271.0 3.4 collective-permute-done.40
  283.8 2.0 collective-permute-start.60
  286.0 3.0 collective-permute-done.52
  294.8 4.0 %collective-permute-done.54 = bf16[2,2,1,1,24,1024]{5,4,3,2,1,0:T(8,128)(2,1)S(1)} collective-permute-done((bf16[2,2,1,1,24,1024]{5,4,3,2,1,0:T(8,128)(2,1)S(1)}, bf16[2,2,1,1,24,1024]{5,4,3,2,1,0:T(8,128)(2,1)S(1)}, u32[]{:S(2)}, u32[]{:S(2)}) %collective-permute-start.54) | collective-permute-done | bytes 196640 | tf_op jit(solution)/shard_map/ppermute | solution.py:952
  306.8 3.4 collective-permute-start.66
  311.2 2.9 collective-permute-start.64
  314.4 2.9 collective-permute-start.62
  318.0 3.1 collective-permute-done.62
  (379 shorter events, 119.3 us)
Async XLA Ops:
  7.2 91.5 %all-gather.4.cloned.1.call-start = ((), (), s32[]{:S(2)}) async-start(), calls=%async_computation | async-start | bytes 2211840 | tf_op jit(solution)/shard_map/all_gather | solution.py:1079
  8.8 27.6 %collective-permute-start.1 = (bf16[1,1,1,1,24,2688]{5,4,3,2,1,0:T(8,128)(2,1)}, bf16[1,1,1,1,24,2688]{5,4,3,2,1,0:T(8,128)(2,1)S(1)}, u32[]{:S(2)}, u32[]{:S(2)}) collective-permute-start(bf16[1,1,1,1,24,2688]{5,4,3,2,1,0:T(8,128)(2,1)} %bitcast.192), channel_id=1, source_target_pairs={{0,8},{1,9},{2,10},{3,11},{4,12},{5,13},{6,14},{7,15},{8,0},{9,1},... | collective-permute-start | bytes 387080 | tf_op jit(solution)/shard_map/ppermute | solution.py:952
  15.6 20.8 %collective-permute-start.2 = (bf16[1,1,1,1,24,896]{5,4,0,1,3,2:T(8,128)(2,1)}, bf16[1,1,1,1,24,896]{5,4,0,1,3,2:T(8,128)(2,1)S(1)}, u32[]{:S(2)}, u32[]{:S(2)}) collective-permute-start(bf16[1,1,1,1,24,896]{5,4,0,1,3,2:T(8,128)(2,1)} %bitcast.202), channel_id=1, source_target_pairs={{0,8},{1,9},{2,10},{3,11},{4,12},{5,13},{6,14},{7,15},{8,0},{9,1},... | collective-permute-start | bytes 129032 | tf_op jit(solution)/shard_map/ppermute | solution.py:952
  15.6 20.8 %collective-permute-start.3 = (bf16[1,1,1,1,96,384]{5,4,0,1,3,2:T(8,128)(2,1)}, bf16[1,1,1,1,96,384]{5,4,0,1,3,2:T(8,128)(2,1)S(1)}, u32[]{:S(2)}, u32[]{:S(2)}) collective-permute-start(bf16[1,1,1,1,96,384]{5,4,0,1,3,2:T(8,128)(2,1)} %bitcast.214), channel_id=1, source_target_pairs={{0,8},{1,9},{2,10},{3,11},{4,12},{5,13},{6,14},{7,15},{8,0},{9,1},... | collective-permute-start | bytes 221192 | tf_op jit(solution)/shard_map/ppermute | solution.py:952
  48.5 13.8 %collective-permute-start.7 = (bf16[2,2,1,1,24,2688]{5,4,3,2,1,0:T(8,128)(2,1)S(1)}, bf16[2,2,1,1,24,2688]{5,4,3,2,1,0:T(8,128)(2,1)S(1)}, u32[]{:S(2)}, u32[]{:S(2)}) collective-permute-start(bf16[2,2,1,1,24,2688]{5,4,3,2,1,0:T(8,128)(2,1)S(1)} %maximum_select_fusion.6), channel_id=1, source_target_pairs={{0,1},{1,0},{2,3},{3,2},{4,5},{5,4},{6,7},{7,6},{8,9},{9,8},{10,11... | collective-permute-start | bytes 1548296 | tf_op jit(solution)/shard_map/ppermute | solution.py:952
  62.6 31.9 %collective-permute-start.10 = (bf16[2,2,1,2,24,2688]{5,4,3,2,1,0:T(8,128)(2,1)S(1)}, bf16[2,2,1,2,24,2688]{5,4,3,2,1,0:T(8,128)(2,1)S(1)}, u32[]{:S(2)}, u32[]{:S(2)}) collective-permute-start(bf16[2,2,1,2,24,2688]{5,4,3,2,1,0:T(8,128)(2,1)S(1)} %maximum_select_fusion.2), channel_id=1, source_target_pairs={{0,2},{1,3},{2,0},{3,1},{4,6},{5,7},{6,4},{7,5},{8,10},{9,11},{10,... | collective-permute-start | bytes 3096584 | tf_op jit(solution)/shard_map/ppermute | solution.py:952
  64.3 28.1 %collective-permute-start.12 = (bf16[2,2,2,1,96,384]{5,4,0,1,3,2:T(8,128)(2,1)S(1)}, bf16[2,2,2,1,96,384]{5,4,0,1,3,2:T(8,128)(2,1)}, u32[]{:S(2)}, u32[]{:S(2)}) collective-permute-start(bf16[2,2,2,1,96,384]{5,4,0,1,3,2:T(8,128)(2,1)S(1)} %maximum_select_fusion.4), channel_id=1, source_target_pairs={{0,1},{1,0},{2,3},{3,2},{4,5},{5,4},{6,7},{7,6},{8,9},{9,8},{10,11... | collective-permute-start | bytes 1769480 | tf_op jit(solution)/shard_map/ppermute | solution.py:952
  65.1 27.4 %collective-permute-start.11 = (bf16[2,2,2,1,24,896]{5,4,0,1,3,2:T(8,128)(2,1)S(1)}, bf16[2,2,2,1,24,896]{5,4,0,1,3,2:T(8,128)(2,1)S(1)}, u32[]{:S(2)}, u32[]{:S(2)}) collective-permute-start(bf16[2,2,2,1,24,896]{5,4,0,1,3,2:T(8,128)(2,1)S(1)} %maximum_select_fusion.7), channel_id=1, source_target_pairs={{0,1},{1,0},{2,3},{3,2},{4,5},{5,4},{6,7},{7,6},{8,9},{9,8},{10,11... | collective-permute-start | bytes 1032200 | tf_op jit(solution)/shard_map/ppermute | solution.py:952
  96.2 21.9 %collective-permute-start.13 = (bf16[384,2688]{1,0:T(8,128)(2,1)}, bf16[384,2688]{1,0:T(8,128)(2,1)}, u32[]{:S(2)}, u32[]{:S(2)}) collective-permute-start(bf16[384,2688]{1,0:T(8,128)(2,1)} %bitcast.32.refs_4_.refs_3_.refs_9_.refs_2_), channel_id=1, source_target_pairs={{0,16},{16,0},{1,17},{17,1},{2,18},{18,2},{3,19},{19,3},{4,20},{20... | collective-permute-start | bytes 6193160 | tf_op jit(solution)/shard_map/ppermute | solution.py:937
  98.1 30.0 %collective-permute-start.16 = (bf16[1536,384]{1,0:T(8,128)(2,1)S(1)}, bf16[1536,384]{1,0:T(8,128)(2,1)}, u32[]{:S(2)}, u32[]{:S(2)}) collective-permute-start(bf16[1536,384]{1,0:T(8,128)(2,1)S(1)} %bitcast.187), channel_id=1, source_target_pairs={{0,16},{16,0},{1,17},{17,1},{2,18},{18,2},{3,19},{19,3},{4,20},{20... | collective-permute-start | bytes 3538952 | tf_op jit(solution)/shard_map/ppermute | solution.py:937
  103.2 14.3 %collective-permute-start.14 = (bf16[384,896]{1,0:T(8,128)(2,1)S(1)}, bf16[384,896]{1,0:T(8,128)(2,1)}, u32[]{:S(2)}, u32[]{:S(2)}) collective-permute-start(bf16[384,896]{1,0:T(8,128)(2,1)S(1)} %bitcast.195), channel_id=1, source_target_pairs={{0,16},{16,0},{1,17},{17,1},{2,18},{18,2},{3,19},{19,3},{4,20},{20... | collective-permute-start | bytes 2064392 | tf_op jit(solution)/shard_map/ppermute | solution.py:937
  167.7 17.1 %collective-permute-start.18 = (bf16[384,768]{1,0:T(8,128)(2,1)S(1)}, bf16[384,768]{1,0:T(8,128)(2,1)S(1)}, u32[]{:S(2)}, u32[]{:S(2)}) collective-permute-start(bf16[384,768]{1,0:T(8,128)(2,1)S(1)} %copy-done.44), channel_id=1, source_target_pairs={{0,16},{16,0},{1,17},{17,1},{2,18},{18,2},{3,19},{19,3},{4,20},{20... | collective-permute-start | bytes 1769480 | tf_op jit(solution)/shard_map/ppermute | solution.py:937
  168.1 16.7 %collective-permute-start.19 = (bf16[16,48,384]{2,1,0:T(8,128)(2,1)S(1)}, bf16[16,48,384]{2,1,0:T(8,128)(2,1)S(1)}, u32[]{:S(2)}, u32[]{:S(2)}) collective-permute-start(bf16[16,48,384]{2,1,0:T(8,128)(2,1)S(1)} %fusion.3), channel_id=1, source_target_pairs={{0,16},{16,0},{1,17},{17,1},{2,18},{18,2},{3,19},{19,3},{4,20},{20... | collective-permute-start | bytes 1769480 | tf_op jit(solution)/shard_map/ppermute | solution.py:937
  168.3 16.5 %collective-permute-start.17 = (bf16[512,384]{1,0:T(8,128)(2,1)S(1)}, bf16[512,384]{1,0:T(8,128)(2,1)S(1)}, u32[]{:S(2)}, u32[]{:S(2)}) collective-permute-start(bf16[512,384]{1,0:T(8,128)(2,1)S(1)} %broadcast_select_fusion.2), channel_id=1, source_target_pairs={{0,16},{16,0},{1,17},{17,1},{2,18},{18,2},{3,19},{19,3},{4,20},{20... | collective-permute-start | bytes 1179656 | tf_op jit(solution)/shard_map/ppermute | solution.py:937
  194.0 19.2 %collective-permute-start.21 = (bf16[2,2,2,1,24,768]{5,4,3,2,1,0:T(8,128)(2,1)S(1)}, bf16[2,2,2,1,24,768]{5,4,3,2,1,0:T(8,128)(2,1)}, u32[]{:S(2)}, u32[]{:S(2)}) collective-permute-start(bf16[2,2,2,1,24,768]{5,4,3,2,1,0:T(8,128)(2,1)S(1)} %dynamic-slice_convert_fusion.7), channel_id=1, source_target_pairs={{0,1},{1,0},{2,3},{3,2},{4,5},{5,4},{6,7},{7,6},{8,9},{9,8},{10,11... | collective-permute-start | bytes 884744 | tf_op jit(solution)/shard_map/ppermute | solution.py:952
  195.1 18.1 %collective-permute-start.22 = (bf16[2,2,2,1,48,384]{5,4,3,2,1,0:T(8,128)(2,1)S(1)}, bf16[2,2,2,1,48,384]{5,4,3,2,1,0:T(8,128)(2,1)}, u32[]{:S(2)}, u32[]{:S(2)}) collective-permute-start(bf16[2,2,2,1,48,384]{5,4,3,2,1,0:T(8,128)(2,1)S(1)} %dynamic-slice_convert_fusion.6), channel_id=1, source_target_pairs={{0,1},{1,0},{2,3},{3,2},{4,5},{5,4},{6,7},{7,6},{8,9},{9,8},{10,11... | collective-permute-start | bytes 884744 | tf_op jit(solution)/shard_map/ppermute | solution.py:952
  196.6 21.7 %collective-permute-start.23 = (bf16[2,2,2,1,24,1024]{5,4,3,2,1,0:T(8,128)(2,1)S(1)}, bf16[2,2,2,1,24,1024]{5,4,3,2,1,0:T(8,128)(2,1)S(1)}, u32[]{:S(2)}, u32[]{:S(2)}) collective-permute-start(bf16[2,2,2,1,24,1024]{5,4,3,2,1,0:T(8,128)(2,1)S(1)} %dynamic-slice_convert_fusion.3), channel_id=1, source_target_pairs={{0,1},{1,0},{2,3},{3,2},{4,5},{5,4},{6,7},{7,6},{8,9},{9,8},{10,11... | collective-permute-start | bytes 1179656 | tf_op jit(solution)/shard_map/ppermute | solution.py:952
  197.7 20.6 %collective-permute-start.24 = (bf16[1,1,1,1,2,2304]{5,4,3,2,1,0:T(2,128)(2,1)S(1)}, bf16[1,1,1,1,2,2304]{5,4,3,2,1,0:T(2,128)(2,1)S(1)}, u32[]{:S(2)}, u32[]{:S(2)}) collective-permute-start(bf16[1,1,1,1,2,2304]{5,4,3,2,1,0:T(2,128)(2,1)S(1)} %bitcast.206), channel_id=1, source_target_pairs={{0,1},{1,0},{2,3},{3,2},{4,5},{5,4},{6,7},{7,6},{8,9},{9,8},{10,11... | collective-permute-start | bytes 27656 | tf_op jit(solution)/shard_map/ppermute | solution.py:952
  223.4 21.6 %collective-permute-start.31 = (bf16[2,2,2,1,24,768]{5,4,3,2,1,0:T(8,128)(2,1)S(1)}, bf16[2,2,2,1,24,768]{5,4,3,2,1,0:T(8,128)(2,1)S(1)}, u32[]{:S(2)}, u32[]{:S(2)}) collective-permute-start(bf16[2,2,2,1,24,768]{5,4,3,2,1,0:T(8,128)(2,1)S(1)} %dynamic-slice_convert_fusion.5), channel_id=1, source_target_pairs={{0,1},{1,0},{2,3},{3,2},{4,5},{5,4},{6,7},{7,6},{8,9},{9,8},{10,11... | collective-permute-start | bytes 884744 | tf_op jit(solution)/shard_map/ppermute | solution.py:952
  224.4 20.7 %collective-permute-start.32 = (bf16[2,2,2,1,48,384]{5,4,3,2,1,0:T(8,128)(2,1)S(1)}, bf16[2,2,2,1,48,384]{5,4,3,2,1,0:T(8,128)(2,1)S(1)}, u32[]{:S(2)}, u32[]{:S(2)}) collective-permute-start(bf16[2,2,2,1,48,384]{5,4,3,2,1,0:T(8,128)(2,1)S(1)} %dynamic-slice_convert_fusion.4), channel_id=1, source_target_pairs={{0,1},{1,0},{2,3},{3,2},{4,5},{5,4},{6,7},{7,6},{8,9},{9,8},{10,11... | collective-permute-start | bytes 884744 | tf_op jit(solution)/shard_map/ppermute | solution.py:952
  225.5 19.5 %collective-permute-start.29 = (bf16[2,2,1,1,24,1024]{5,4,3,2,1,0:T(8,128)(2,1)S(1)}, bf16[2,2,1,1,24,1024]{5,4,3,2,1,0:T(8,128)(2,1)S(1)}, u32[]{:S(2)}, u32[]{:S(2)}) collective-permute-start(bf16[2,2,1,1,24,1024]{5,4,3,2,1,0:T(8,128)(2,1)S(1)} %dynamic-slice_convert_fusion.9), channel_id=1, source_target_pairs={{0,2},{1,3},{2,0},{3,1},{4,6},{5,7},{6,4},{7,5},{8,10},{9,11},{10,... | collective-permute-start | bytes 589832 | tf_op jit(solution)/shard_map/ppermute | solution.py:952
  227.0 18.0 %collective-permute-start.27 = (bf16[2,2,1,1,24,768]{5,4,3,2,1,0:T(8,128)(2,1)S(1)}, bf16[2,2,1,1,24,768]{5,4,3,2,1,0:T(8,128)(2,1)S(1)}, u32[]{:S(2)}, u32[]{:S(2)}) collective-permute-start(bf16[2,2,1,1,24,768]{5,4,3,2,1,0:T(8,128)(2,1)S(1)} %dynamic-slice_convert_fusion.13), channel_id=1, source_target_pairs={{0,2},{1,3},{2,0},{3,1},{4,6},{5,7},{6,4},{7,5},{8,10},{9,11},{10,... | collective-permute-start | bytes 442376 | tf_op jit(solution)/shard_map/ppermute | solution.py:952
  227.6 17.5 %collective-permute-start.28 = (bf16[2,2,1,1,48,384]{5,4,3,2,1,0:T(8,128)(2,1)S(1)}, bf16[2,2,1,1,48,384]{5,4,3,2,1,0:T(8,128)(2,1)S(1)}, u32[]{:S(2)}, u32[]{:S(2)}) collective-permute-start(bf16[2,2,1,1,48,384]{5,4,3,2,1,0:T(8,128)(2,1)S(1)} %dynamic-slice_convert_fusion.12), channel_id=1, source_target_pairs={{0,2},{1,3},{2,0},{3,1},{4,6},{5,7},{6,4},{7,5},{8,10},{9,11},{10,... | collective-permute-start | bytes 442376 | tf_op jit(solution)/shard_map/ppermute | solution.py:952
  254.4 20.1 %collective-permute-start.37 = (bf16[384,1024]{1,0:T(8,128)(2,1)S(1)}, bf16[384,1024]{1,0:T(8,128)(2,1)S(1)}, u32[]{:S(2)}, u32[]{:S(2)}) collective-permute-start(bf16[384,1024]{1,0:T(8,128)(2,1)S(1)} %copy-done.43), channel_id=1, source_target_pairs={{0,16},{16,0},{1,17},{17,1},{2,18},{18,2},{3,19},{19,3},{4,20},{20... | collective-permute-start | bytes 2359304 | tf_op jit(solution)/shard_map/ppermute | solution.py:937
  255.3 19.1 %collective-permute-start.42 = (bf16[2,2,1,1,24,768]{5,4,3,2,1,0:T(8,128)(2,1)S(1)}, bf16[2,2,1,1,24,768]{5,4,3,2,1,0:T(8,128)(2,1)S(1)}, u32[]{:S(2)}, u32[]{:S(2)}) collective-permute-start(bf16[2,2,1,1,24,768]{5,4,3,2,1,0:T(8,128)(2,1)S(1)} %dynamic-slice_convert_fusion.11), channel_id=1, source_target_pairs={{0,2},{1,3},{2,0},{3,1},{4,6},{5,7},{6,4},{7,5},{8,10},{9,11},{10,... | collective-permute-start | bytes 442376 | tf_op jit(solution)/shard_map/ppermute | solution.py:952
  255.9 18.6 %collective-permute-start.43 = (bf16[2,2,1,1,48,384]{5,4,3,2,1,0:T(8,128)(2,1)S(1)}, bf16[2,2,1,1,48,384]{5,4,3,2,1,0:T(8,128)(2,1)S(1)}, u32[]{:S(2)}, u32[]{:S(2)}) collective-permute-start(bf16[2,2,1,1,48,384]{5,4,3,2,1,0:T(8,128)(2,1)S(1)} %dynamic-slice_convert_fusion.10), channel_id=1, source_target_pairs={{0,2},{1,3},{2,0},{3,1},{4,6},{5,7},{6,4},{7,5},{8,10},{9,11},{10,... | collective-permute-start | bytes 442376 | tf_op jit(solution)/shard_map/ppermute | solution.py:952
  275.2 27.6 %collective-permute-start.61 = (bf16[2,1,1,1,48,384]{5,4,3,2,1,0:T(8,128)(2,1)}, bf16[2,1,1,1,48,384]{5,4,3,2,1,0:T(8,128)(2,1)}, u32[]{:S(2)}, u32[]{:S(2)}) collective-permute-start(bf16[2,1,1,1,48,384]{5,4,3,2,1,0:T(8,128)(2,1)} %dynamic-slice_convert_fusion.16), channel_id=1, source_target_pairs={{0,4},{1,5},{2,6},{3,7},{4,0},{5,1},{6,2},{7,3},{8,12},{9,13},{10,... | collective-permute-start | bytes 221192 | tf_op jit(solution)/shard_map/ppermute | solution.py:952
  283.8 19.0 %collective-permute-start.60 = (bf16[2,1,1,1,24,768]{5,4,3,2,1,0:T(8,128)(2,1)}, bf16[2,1,1,1,24,768]{5,4,3,2,1,0:T(8,128)(2,1)}, u32[]{:S(2)}, u32[]{:S(2)}) collective-permute-start(bf16[2,1,1,1,24,768]{5,4,3,2,1,0:T(8,128)(2,1)} %dynamic-slice_convert_fusion.17), channel_id=1, source_target_pairs={{0,4},{1,5},{2,6},{3,7},{4,0},{5,1},{6,2},{7,3},{8,12},{9,13},{10,... | collective-permute-start | bytes 221192 | tf_op jit(solution)/shard_map/ppermute | solution.py:952
  317.9 14.1 %collective-permute-start.44 = (f32[512,384]{1,0:T(8,128)}, f32[512,384]{1,0:T(8,128)S(1)}, u32[]{:S(2)}, u32[]{:S(2)}) collective-permute-start(f32[512,384]{1,0:T(8,128)} %broadcast_select_fusion), channel_id=1, source_target_pairs={{0,16},{16,0},{1,17},{17,1},{2,18},{18,2},{3,19},{19,3},{4,20},{20... | collective-permute-start | bytes 2359304 | tf_op jit(solution)/shard_map/ppermute | solution.py:937
  321.7 15.2 %collective-permute-start.71 = (f32[48,384]{1,0:T(8,128)}, f32[48,384]{1,0:T(8,128)}, u32[]{:S(2)}, u32[]{:S(2)}) collective-permute-start(f32[48,384]{1,0:T(8,128)} %select_bitcast_fusion.5), channel_id=1, source_target_pairs={{0,16},{16,0},{1,17},{17,1},{2,18},{18,2},{3,19},{19,3},{4,20},{20... | collective-permute-start | bytes 221192 | tf_op jit(solution)/shard_map/ppermute | solution.py:937
  322.4 13.0 %collective-permute-start.70 = (f32[24,768]{1,0:T(8,128)}, f32[24,768]{1,0:T(8,128)}, u32[]{:S(2)}, u32[]{:S(2)}) collective-permute-start(f32[24,768]{1,0:T(8,128)} %select_bitcast_fusion.6), channel_id=1, source_target_pairs={{0,16},{16,0},{1,17},{17,1},{2,18},{18,2},{3,19},{19,3},{4,20},{20... | collective-permute-start | bytes 221192 | tf_op jit(solution)/shard_map/ppermute | solution.py:937
  324.2 14.4 %collective-permute-start.69 = (f32[24,1024]{1,0:T(8,128)}, f32[24,1024]{1,0:T(8,128)}, u32[]{:S(2)}, u32[]{:S(2)}) collective-permute-start(f32[24,1024]{1,0:T(8,128)} %select_bitcast_fusion.4), channel_id=1, source_target_pairs={{0,16},{16,0},{1,17},{17,1},{2,18},{18,2},{3,19},{19,3},{4,20},{20... | collective-permute-start | bytes 294920 | tf_op jit(solution)/shard_map/ppermute | solution.py:937
  (89 other events, 793.9 us)
Sparse Core Ops, SparseCore 0:
  36.5 44.3 all-gather.3
where the time goes:
time: 355 us; the launch traced here: 350 us
  Pallas kernels  109 us (31%)
  waiting for transfers between devices  79.9 us (23%)
  starting transfers between devices  70.8 us (20%)
  other arithmetic  29.4 us (8%)
  local copies, waits for them, and re-layouts  21.2 us (6%)
  blocking collectives  17.8 us (5%)
  between operations  15.6 us (4%)
  matrix products  5.3 us (1%)
    pallas_call x10, Pallas kernels, call(): pl.pallas_call(kernel, out_shape=[jax.ShapeDtypeStruct(shape, kind) for s...  105 us
    ppermute x52, waiting for transfers between devices, partner(): return lax.ppermute(values, 'row', [(i, i ^ 1 << bit) for i in range(size)])  78.1 us
    ppermute x52, starting transfers between devices, partner(): return lax.ppermute(values, 'row', [(i, i ^ 1 << bit) for i in range(size)])  66.6 us
    all_gather x1, blocking collectives, on_device(): lax.all_gather(w_ada[0], 'row', axis_index_groups=groups(along_z), tiled=...  17.8 us
    unnamed x105, local copies, waits for them, and re-layouts  8.72 us
    select_n x24, other arithmetic, join(): jnp.where(bit_of(bit) == 0, jnp.concatenate([held, other], axis=axis_of(b...  7.43 us
  transfers between devices with their start and end apart: 73, of which 23 were waited for; matrix products, arithmetic and copies ran while one was open for 13% of the time, Pallas kernels for 20%

commit v1 on v0

--- a/solution.py
+++ b/solution.py
@@ -713,7 +713,7 @@
         + [pltpu.VMEM(shape, kind) for shape, kind, _ in outs.values()]
         + [pltpu.VMEM(shape, kind) for shape, kind in scratch.values()]
         + [pltpu.SemaphoreType.DMA((len(ins),)), pltpu.SemaphoreType.DMA((len(outs),))],
-        compiler_params=pltpu.CompilerParams(vmem_limit_bytes=56 * 1024 * 1024),
+        compiler_params=pltpu.CompilerParams(vmem_limit_bytes=44 * 1024 * 1024),
         cost_estimate=pl.CostEstimate(flops=flops, bytes_accessed=4 << 20, transcendentals=0),
     )(layouts, *arrays)
 
@@ -733,6 +733,11 @@
 AT_UP = (0, FF)
 AT_QK = (FF, FF + 2 * D)
 AT_OUT = (FF + 2 * D, FF + 3 * D)
+ADA_CUT = 1024
+AT_ADA_A = (FF + 3 * D, FF + 3 * D + ADA_CUT)
+AT_LIFTED = FF + 3 * D + ADA_CUT
+AT_VGD = (0, 2 * D + LANES)
+AT_ADA_B = (2 * D + LANES, 8 * D + LANES - ADA_CUT)
 
 
 def attn_forward(layer, layouts, x, mods, small, packed, vgd):
@@ -744,7 +749,7 @@
             x=micro(x),
             mods=own(mods),
             w_qk=own(packed, AT_QK),
-            w_vgd=own(vgd),
+            w_vgd=own(vgd, AT_VGD),
             small=own(small),
         ),
         dict(
@@ -873,7 +878,7 @@
         dict(
             low=plain(low),
             w_qk=own(packed, AT_QK),
-            w_vgd=own(vgd),
+            w_vgd=own(vgd, AT_VGD),
             x=micro(x),
             mid_grad=plain(mid_grad),
             mods=own(mods),
@@ -912,29 +917,220 @@
     )(b_up, b_down, taps, b_decay)
 
 
-def pack_kernel(*refs):
-    packed = refs[-1]
-    at = 0
-    for ref in refs[:-1]:
-        width = ref.shape[1]
-        if width % LANES:
-            packed[:, at:] = jnp.zeros((packed.shape[0], packed.shape[1] - at), packed.dtype)
-        packed[:, at : at + width] = ref[...]
-        at += width
-
-
-def pack(*arrays):
-    total = sum(-(-array.shape[1] // LANES) * LANES for array in arrays)
+def padded(width):
+    return -(-width // LANES) * LANES
+
+
+def pack_kernel(groups, *refs):
+    sources, packed = list(refs[: sum(groups)]), refs[sum(groups) :]
+    for count, target in zip(groups, packed):
+        at = 0
+        for _ in range(count):
+            ref = sources.pop(0)
+            width = ref.shape[1]
+            if width % LANES:
+                zeros = jnp.zeros((target.shape[0], padded(width)), target.dtype)
+                target[:, at : at + padded(width)] = zeros
+            target[:, at : at + width] = ref[...]
+            at += padded(width)
+
+
+def pack(*groups):
+    arrays = [array for group in groups for array in group]
     return pl.pallas_call(
-        pack_kernel,
-        out_shape=jax.ShapeDtypeStruct((arrays[0].shape[0], total), arrays[0].dtype),
+        functools.partial(pack_kernel, [len(group) for group in groups]),
+        out_shape=[
+            jax.ShapeDtypeStruct(
+                (group[0].shape[0], sum(padded(array.shape[1]) for array in group)), bf16
+            )
+            for group in groups
+        ],
         in_specs=[VMEM] * len(arrays),
+        out_specs=[VMEM] * len(groups),
+    )(*arrays)
+
+
+def mods_kernel(conditions, bias, packed, vgd, out, ada_a, ada_b, sems):
+    copies = [
+        pltpu.make_async_copy(packed.at[:, AT_ADA_A[0] : AT_ADA_A[1]], ada_a, sems.at[0]),
+        pltpu.make_async_copy(vgd.at[:, AT_ADA_B[0] : AT_ADA_B[1]], ada_b, sems.at[1]),
+    ]
+    for copy in copies:
+        copy.start()
+    values = conditions[...].astype(f32)
+    lifted = (values * sigmoid(values)).astype(bf16)
+    for copy in copies:
+        copy.wait()
+    out[...] = jnp.concatenate([mm(lifted, ada_a[...]), mm(lifted, ada_b[...])], axis=1) + bias[...]
+
+
+ADA_SCRATCH = [
+    pltpu.VMEM((D, ADA_CUT), bf16),
+    pltpu.VMEM((D, 6 * D - ADA_CUT), bf16),
+    pltpu.SemaphoreType.DMA((2,)),
+]
+
+
+def modulations(conditions, bias, packed, vgd):
+    return pl.pallas_call(
+        mods_kernel,
+        out_shape=jax.ShapeDtypeStruct((MICRO * SLOTS, 6 * D), f32),
+        in_specs=[VMEM, VMEM, ANY, ANY],
         out_specs=VMEM,
-    )(*arrays)
+        scratch_shapes=ADA_SCRATCH,
+        compiler_params=pltpu.CompilerParams(vmem_limit_bytes=16 * 1024 * 1024),
+        cost_estimate=pl.CostEstimate(flops=10**9, bytes_accessed=2 << 20, transcendentals=0),
+    )(conditions, bias, packed, vgd)
+
+
+def lifted_kernel(mod_low, packed, vgd, out, ada_a, ada_b, sems):
+    copies = [
+        pltpu.make_async_copy(packed.at[:, AT_ADA_A[0] : AT_ADA_A[1]], ada_a, sems.at[0]),
+        pltpu.make_async_copy(vgd.at[:, AT_ADA_B[0] : AT_ADA_B[1]], ada_b, sems.at[1]),
+    ]
+    for copy in copies:
+        copy.start()
+    for copy in copies:
+        copy.wait()
+    grad = mod_low[...]
+    out[...] = mm_t(grad[:, :ADA_CUT], ada_a[...]) + mm_t(grad[:, ADA_CUT:], ada_b[...])
+
+
+def lifted_grads(mod_low, packed, vgd):
+    return pl.pallas_call(
+        lifted_kernel,
+        out_shape=jax.ShapeDtypeStruct((MICRO * SLOTS, D), f32),
+        in_specs=[VMEM, ANY, ANY],
+        out_specs=VMEM,
+        scratch_shapes=ADA_SCRATCH,
+        compiler_params=pltpu.CompilerParams(vmem_limit_bytes=16 * 1024 * 1024),
+        cost_estimate=pl.CostEstimate(flops=10**9, bytes_accessed=2 << 20, transcendentals=0),
+    )(mod_low, packed, vgd)
+
+
+def step_kernel(bit, count, *refs):
+    mine = (lax.axis_index("row") >> bit) & 1
+    kept, came, stays, goes = (refs[i * count : (i + 1) * count] for i in range(4))
+    for i in range(count):
+        stays[i][...] = kept[i][:, mine] + came[i][:, mine].astype(f32)
+        goes[i][...] = (kept[i][:, 1 - mine] + came[i][:, 1 - mine].astype(f32)).astype(bf16)
+
+
+def step(kept, came, bit):
+    count = len(kept)
+    paired = lambda array: array.reshape((array.shape[0] // 2, 2) + array.shape[1:])
+    kept = [paired(array) for array in kept]
+    came = [paired(array) for array in came]
+    shapes = [array.shape[:1] + array.shape[2:] for array in kept]
+    size = sum(array.size for array in kept)
+    out = pl.pallas_call(
+        functools.partial(step_kernel, bit, count),
+        out_shape=[jax.ShapeDtypeStruct(shape, f32) for shape in shapes]
+        + [jax.ShapeDtypeStruct(shape, bf16) for shape in shapes],
+        in_specs=[VMEM] * (2 * count),
+        out_specs=[VMEM] * (2 * count),
+        compiler_params=pltpu.CompilerParams(vmem_limit_bytes=24 * 1024 * 1024),
+        cost_estimate=pl.CostEstimate(flops=size, bytes_accessed=8 * size, transcendentals=0),
+    )(*kept, *came)
+    return list(out[:count]), list(out[count:])
+
+
+def output_kernel(*refs):
+    first = lax.axis_index("section") == 0
+    ins, outs = refs[:20], refs[20:]
+
+    def chosen(number):
+        one, two, one_came, two_came = (ins[4 * number + i][...] for i in range(4))
+        return jnp.where(first, one, two), jnp.where(first, one_came, two_came)
+
+    def halves(number):
+        mine, other = chosen(number)
+        return jnp.where(first, mine, other), jnp.where(first, other, mine)
+
+    attn = halves(0)
+    cut = GROUP - 2 * D
+    outs[0][...] = attn[0][:, :D]
+    outs[1][...] = attn[0][:, D : 2 * D]
+    outs[2][:, :cut] = attn[0][:, 2 * D :]
+    outs[2][:, cut:] = attn[1][:, : D - cut]
+    outs[3][...] = attn[1][:, D - cut : 2 * D - cut]
+    outs[4][...] = attn[1][:, 2 * D - cut : 3 * D - cut]
+    outs[5][...] = attn[1][:, 3 * D - cut : 3 * D - cut + HEADS]
+    up = halves(1)
+    outs[6][:, : FF // 2] = up[0]
+    outs[6][:, FF // 2 :] = up[1]
+    down = halves(2)
+    outs[7][0] = down[0]
+    outs[7][1] = down[1]
+    mine, other = chosen(3)
+    outs[8][...] = mine + other
+    mine, other = chosen(4)
+    small = mine + other
+    half = 2 * D
+    for i in range(3):
+        outs[9][:, i * half : (i + 1) * half] = small[i : i + 1, :]
+    for i in range(2):
+        outs[10][:, i * half : (i + 1) * half] = small[3 + i : 4 + i, :]
+    outs[11][...] = small[5:6, :D]
+    outs[12][0:1, :] = small[5:6, D:]
+    outs[12][1:2, :] = small[6:7, :D]
+    outs[12][2:3, :] = small[6:7, D:]
+    outs[13][...] = small[7:8, :HEADS]
+
+
+def outputs(quads, shard, down_rows):
+    shapes = (
+        [(shard, D)] * 5
+        + [(shard, HEADS), (shard, FF), (2, down_rows, D), (shard, 6 * D)]
+        + [(1, 6 * D), (1, FF), (1, D), (3, D), (1, HEADS)]
+    )
+    flat_in = [array for quad in quads for array in quad]
+    return pl.pallas_call(
+        output_kernel,
+        out_shape=[jax.ShapeDtypeStruct(shape, f32) for shape in shapes],
+        in_specs=[VMEM] * len(flat_in),
+        out_specs=[VMEM] * len(shapes),
+    )(*flat_in)
+
+
+def both_kernel(one, two, one_came, two_came, out, sems):
+    section = lax.axis_index("section")
+
+    def move(mine, came, layer):
+        copies = [
+            pltpu.make_async_copy(mine, out.at[layer], sems.at[0]),
+            pltpu.make_async_copy(came, out.at[1 - layer], sems.at[1]),
+        ]
+        for copy in copies:
+            copy.start()
+        for copy in copies:
+            copy.wait()
+
+    @pl.when(section == 0)
+    def _():
+        move(one, one_came, 0)
+
+    @pl.when(section == 1)
+    def _():
+        move(two, two_came, 1)
+
+
+def both_micros(one, two, one_came, two_came):
+    return pl.pallas_call(
+        both_kernel,
+        out_shape=jax.ShapeDtypeStruct((MICRO,) + one.shape, one.dtype),
+        in_specs=[ANY] * 4,
+        out_specs=ANY,
+        scratch_shapes=[pltpu.SemaphoreType.DMA((2,))],
+    )(one, two, one_came, two_came)
 
 
 def swap(values):
     return lax.ppermute(values, "section", [(0, 1), (1, 0)])
+
+
+def hand(values, source):
+    return lax.ppermute(values, "section", [(source, 1 - source)])
 
 
 def row_bits():
@@ -976,37 +1172,8 @@
     return held.reshape(-1, held.shape[-1])
 
 
-def by_bits(values):
-    bits = lax.axis_size("row").bit_length() - 1
-    return values.reshape((2,) * bits + values.shape[1:])
-
-
-def cut(held, bit):
-    axis = axis_of(bit)
-    mine = bit_of(bit)
-    sent = lax.dynamic_index_in_dim(held, 1 - mine, axis, keepdims=True)
-    kept = lax.dynamic_index_in_dim(held, mine, axis, keepdims=True)
-    return sent, kept
-
-
 def lock(*arrays):
     return lax.optimization_barrier(arrays)
-
-
-class Scatter:
-    def __init__(self, values):
-        self.held = by_bits(values)
-        self.kept = None
-
-    def ready(self, bit):
-        sent, self.kept = cut(self.held, bit)
-        return sent.astype(bf16)
-
-    def take(self, other):
-        self.held = self.kept + other.astype(f32)
-
-    def result(self):
-        return self.held.reshape(self.held.shape[-2:])
 
 
 class Gather:
@@ -1056,31 +1223,17 @@
     shard = w_query.shape[1]
     along_x, along_y, along_z = row_bits()
     plane = along_x + along_y
-    every = plane + along_z
-
-    def pick(pair):
-        return jnp.where(is_first, pair[0], pair[1])
-
-    def pick_other(pair):
-        return jnp.where(is_first, pair[1], pair[0])
 
     def both(values):
         return values, swap(values)
 
-    def groups(run):
-        rest = [bit for bit in every if bit not in run]
-        numbers = lambda bits: [
-            sum(((i >> place) & 1) << bit for place, bit in enumerate(bits))
-            for i in range(1 << len(bits))
-        ]
-        return [[base + step for step in numbers(run)] for base in numbers(rest)]
-
-    ada = lax.all_gather(w_ada[0], "row", axis_index_groups=groups(along_z), tiled=True)
-    ada = lax.all_gather(ada, "row", axis_index_groups=groups(plane), tiled=True)
-    height, width = 1 << len(along_z), 1 << len(plane)
-
-    group_a = [Gather(pack(w_up[0], w_query[0], w_key[0], w_out[0]))]
-    group_b = [Gather(pack(w_value[0], w_gate[0], w_decay[0])), Gather(w_down[0])]
+    lifted_own = jax.nn.silu(conditions.astype(f32)).astype(bf16)
+    group_a, group_b = pack(
+        (w_up[0], w_query[0], w_key[0], w_out[0], w_ada[0, :, :ADA_CUT], lifted_own.reshape(shard, -1)),
+        (w_value[0], w_gate[0], w_decay[0], w_ada[0, :, ADA_CUT:]),
+    )
+    group_a = [Gather(group_a)]
+    group_b = [Gather(group_b), Gather(w_down[0])]
     chains = group_a + group_b
     for bit in reversed(along_z):
         end(chains, lock(*send(begin(chains, bit), bit)))
@@ -1091,18 +1244,10 @@
         end(chains, others)
     packed, vgd, down = [both(flat(chain.held)) for chain in chains]
 
-    lifted_own = jax.nn.silu(conditions.astype(f32)).astype(bf16).reshape(MICRO * SLOTS, D)
-    lifted_cut = lifted_own.reshape(MICRO * SLOTS, height, width, shard).swapaxes(1, 2)
-    mods = both(mm(lifted_cut.reshape(MICRO * SLOTS, D), ada) + b_ada[0])
+    mods = both(
+        modulations(conditions.reshape(MICRO * SLOTS, D), b_ada, packed[0], vgd[0])
+    )
     smalls = both(pack_small(b_up, b_down, conv_kernel, b_decay))
-
-    late, _ = lock(lifted_own, mods[0])
-    lifted_rows = Gather(late)
-    for bit in reversed(every):
-        end([lifted_rows], send(begin([lifted_rows], bit), bit))
-    lifted_rows = lax.dynamic_slice_in_dim(
-        flat(lifted_rows.held), lax.axis_index("row") * shard, shard, 1
-    )
 
     x = tokens
     kept = []
@@ -1116,34 +1261,25 @@
 
     def ffn_step(l, grad):
         x, saved, gated, branch, down_raw = kept[l]
-        mid_grad, branch_low, gwo, keep, sent, gwn, sums = ffn_backward(
+        mid_grad, branch_low, gwo, up_keep, up_send, gwn, sums = ffn_backward(
             l, layouts, x, mods, smalls, gated, branch, down_raw, grad, packed, down
         )
         pair = gwn.reshape(devices, 2, FF // devices // 2, D)
         down_keep = lax.dynamic_index_in_dim(pair, section, 1, keepdims=False)
         down_send = lax.dynamic_index_in_dim(pair, 1 - section, 1, keepdims=False).astype(bf16)
-        return (branch_low, gwo), mid_grad, (sent, down_send), (keep, down_keep), sums
+        keep = [up_keep.reshape(devices, shard, FF // 2), down_keep]
+        sent = [up_send.reshape(devices, shard, FF // 2), down_send]
+        return [branch_low, gwo], mid_grad, keep, sent, sums
 
     def mixer_step(l, carried):
-        return mixer_backward(l, layouts, smalls, kept[l][1], *carried, packed)
+        low, keep, sent, sums = mixer_backward(l, layouts, smalls, kept[l][1], *carried, packed)
+        by_row = lambda array: [array.reshape(devices, shard, GROUP)]
+        return low, by_row(keep), by_row(sent), sums
 
     def input_step(l, low, mid_grad, ffn_sums, mixer_sums):
         return input_backward(
             l, layouts, kept[l][0], mods, low, mid_grad, ffn_sums, mixer_sums, packed, vgd
         )
-
-    def ffn_chains(keep, others):
-        up_half = keep[0] + others[0].astype(f32)
-        down_half = keep[1] + others[1].astype(f32)
-        return [Scatter(up_half.reshape(devices, shard, FF // 2)), Scatter(down_half)]
-
-    def attn_chain(keep, other):
-        return [Scatter((keep + other.astype(f32)).reshape(devices, shard, GROUP))]
-
-    def steps(chains, bits):
-        for bit in bits[:-1]:
-            end(chains, send(begin(chains, bit), bit))
-        return begin(chains, bits[-1])
 
     def divide(arrays, *counts):
         parts = []
@@ -1152,127 +1288,152 @@
             arrays = arrays[count:]
         return parts
 
+    def run(keep, came, bits):
+        for bit in bits[:-1]:
+            keep, sent = step(keep, came, bit)
+            came = send(sent, bit)
+        return step(keep, came, bits[-1])
+
     x_bits, y_bits, z_bits = along_x, along_y, along_z
-    carried, mid_grad, f2_send, f2_keep, f2_sums = ffn_step(1, output_grad)
-    acts_send = pick_other(acts)
-    *carried, acts_send, s0, s1 = lock(*carried, acts_send, *f2_send)
-    f2_other = [swap(s0), swap(s1)]
-    acts_other = swap(acts_send)
-    low, a2_keep, a2_send, m2_sums = mixer_step(1, carried)
-    low, acts_other, *f2_other = lock(low, acts_other, *f2_other)
-    f2 = ffn_chains(f2_keep, f2_other)
-    f2_sent = steps(f2, x_bits)
-    low, a2_send, *f2_sent = lock(low, a2_send, *f2_sent)
-    f2_other = send(f2_sent, x_bits[-1])
-    a2_other = swap(a2_send)
-    gx_two, grad, mod_low_two, sums_two = input_step(1, low, mid_grad, f2_sums, m2_sums)
-    grad, a2_other, mod_low_two = lock(grad, a2_other, mod_low_two[:SLOTS])
-    a2 = attn_chain(a2_keep, a2_other)
-    mod2 = [Gather(mod_low_two)]
-    a2_sent = steps(a2 + mod2, x_bits)
-    grad, *a2_sent = lock(grad, *a2_sent)
-    a2_other = send(a2_sent, x_bits[-1])
-
-    carried, mid_grad, f1_send, f1_keep, f1_sums = ffn_step(0, grad[None])
-    locked = lock(*carried, *f1_send, *f2_other, *a2_other)
-    carried, f1_send, locked = divide(locked, 2, 2, 4)
-    f1_other = lock(*[swap(array) for array in f1_send])
-    two = f2 + a2 + mod2
-    end(two, locked)
-    two_sent = steps(two, y_bits)
-    f1 = ffn_chains(f1_keep, f1_other)
-    f1_sent = steps(f1, x_bits)
+    carried, mid_grad, f2_keep, f2_sent, f2_sums = ffn_step(1, output_grad)
+    *carried, s0, s1 = lock(*carried, *f2_sent)
+    f2_came = [swap(s0), swap(s1)]
+    acts_came = [hand(acts[0], 1), hand(acts[1], 0)]
+    low, a2_keep, a2_sent, m2_sums = mixer_step(1, carried)
+    low, a2_sent, f2_came, acts_came = divide(lock(low, *a2_sent, *f2_came, *acts_came), 1, 1, 2, 2)
+    a2_came = [swap(a2_sent[0])]
+    gx_two, grad, mod_low_two, sums_two = input_step(1, low[0], mid_grad, f2_sums, m2_sums)
+    grad, gx_two, mod_low_two, *a2_came = lock(grad, gx_two, mod_low_two[:SLOTS], *a2_came)
+    two_keep, two_sent = run(f2_keep + a2_keep, f2_came + a2_came, x_bits)
+    mod_two = Gather(mod_low_two)
+    for bit in x_bits[:-1]:
+        end([mod_two], send(begin([mod_two], bit), bit))
+    grad, gx_two, *two_sent = lock(grad, gx_two, *two_sent, mod_two.ready(x_bits[-1]))
+    two_came = send(two_sent, x_bits[-1])
+    gx_two_came = hand(gx_two, 0)
+
+    carried, mid_grad, f1_keep, f1_sent, f1_sums = ffn_step(0, grad[None])
+    carried, f1_sent, two_came, (mod_came, gx_two_came) = divide(
+        lock(*carried, *f1_sent, *two_came, gx_two_came), 2, 2, 3, 2
+    )
+    f1_came = [swap(array) for array in f1_sent]
+    mod_two.take(mod_came)
+    two_keep, two_sent = run(two_keep, two_came, y_bits)
+    f1_keep, f1_sent = run(f1_keep, f1_came, x_bits)
+    for bit in y_bits[:-1]:
+        end([mod_two], send(begin([mod_two], bit), bit))
+    two_sent = two_sent + [mod_two.ready(y_bits[-1])]
     carried, two_sent, f1_sent = divide(lock(*carried, *two_sent, *f1_sent), 2, 4, 2)
-    two_other = send(two_sent, y_bits[-1])
-    f1_other = send(f1_sent, x_bits[-1])
-    low, a1_keep, a1_send, m1_sums = mixer_step(0, carried)
-    low, *locked = lock(low, *two_other, *f1_other)
-    end(two + f1, locked)
-    two_sent = steps(two, z_bits)
-    f1_sent = steps(f1, y_bits)
-    low, a1_send, *locked = lock(low, a1_send, *two_sent, *f1_sent)
-    two_sent, f1_sent = divide(locked, 4, 2)
-    a1_other = swap(a1_send)
-    two_other = send(two_sent, z_bits[-1])
-    f1_other = send(f1_sent, y_bits[-1])
-    gx_one, _, mod_low_one, sums_one = input_step(0, low, mid_grad, f1_sums, m1_sums)
-    gx_send = pick_other((gx_one, gx_two))
+    two_came = send(two_sent, y_bits[-1])
+    f1_came = send(f1_sent, x_bits[-1])
+    low, a1_keep, a1_sent, m1_sums = mixer_step(0, carried)
+    low, a1_sent, two_came, (mod_came,), f1_came = divide(
+        lock(low, *a1_sent, *two_came, *f1_came), 1, 1, 3, 1, 2
+    )
+    mod_two.take(mod_came)
+    two_keep, two_sent = run(two_keep, two_came, z_bits[:1])
+    f1_keep, f1_sent = run(f1_keep, f1_came, y_bits)
+    two_sent = two_sent + [mod_two.ready(z_bits[0])]
+    low, a1_sent, two_sent, f1_sent = divide(lock(*low, *a1_sent, *two_sent, *f1_sent), 1, 1, 4, 2)
+    a1_came = [swap(a1_sent[0])]
+    two_came = send(two_sent, z_bits[0])
+    f1_came = send(f1_sent, y_bits[-1])
+    gx_one, _, mod_low_one, sums_one = input_step(0, low[0], mid_grad, f1_sums, m1_sums)
     mod_low_one = mod_low_one[:SLOTS]
-    a1_other, mod_low_one, sums_one, gx_send, *locked = lock(
-        a1_other, mod_low_one, sums_one, gx_send, *two_other, *f1_other
-    )
-    end(two + f1, locked)
-    mod1 = [Gather(mod_low_one)]
-    totals = [Total(jnp.concatenate([sums_one, sums_two], axis=0))]
-    one = attn_chain(a1_keep, a1_other) + mod1 + totals
-    gx_other = swap(gx_send)
-    mod_other = swap(pick_other((mod_low_one, mod_low_two)))
-    for bit in plane:
-        end(one, lock(*send(begin(one, bit), bit)))
-    one = one + f1
-    for bit in z_bits:
-        end(one, lock(*send(begin(one, bit), bit)))
-
+    rest = (gx_one, mod_low_one, sums_one)
+    rest, a1_came, two_came, (mod_came,), f1_came = divide(
+        lock(*rest, *a1_came, *two_came, *f1_came), 3, 1, 3, 1, 2
+    )
+    gx_one, mod_low_one, sums_one = rest
+    mod_two.take(mod_came)
+
+    mod_one = Gather(mod_low_one)
+    total = Total(jnp.concatenate([sums_one, sums_two], axis=0))
+    one_keep, one_came = a1_keep, a1_came
+    z_work = [(two_keep, two_came, z_bits[1:], [mod_two]), (f1_keep, f1_came, z_bits, [])]
+    for place, bit in enumerate(plane):
+        one_keep, one_sent = step(one_keep, one_came, bit)
+        sent = lock(*one_sent, mod_one.ready(bit), total.ready(bit))
+        one_came, (mod_came,), (total_came,) = divide(send(sent, bit), 1, 1, 1)
+        if place == 0:
+            gx_one_came = hand(gx_one, 1)
+            mod_came_one, mod_came_two = hand(mod_low_one, 1), hand(mod_low_two, 0)
+        mod_one.take(mod_came)
+        total.take(total_came)
+    two_keep_came = (two_keep, two_came)
+    for place, bit in enumerate(z_bits):
+        keep = one_keep + f1_keep
+        came = one_came + f1_came
+        chains = [mod_one, total]
+        if place:
+            keep, came = keep + two_keep_came[0], came + two_keep_came[1]
+            chains = chains + [mod_two]
+        keep, sent = step(keep, came, bit)
+        ready = [chain.ready(bit) for chain in chains]
+        got = list(lock(*send(lock(*sent, *ready), bit)))
+        came = got[: len(keep)]
+        end(chains, got[len(keep) :])
+        one_keep, f1_keep = keep[:1], keep[1:3]
+        one_came, f1_came = came[:1], came[1:3]
+        if place:
+            two_keep_came = (keep[3:], came[3:])
+    added = [
+        (mine + other.astype(f32)).reshape(mine.shape[-2:]) for mine, other in zip(keep, came)
+    ]
+    a1, up1, down1, up2, down2, a2 = added
+
+    lifted_rows = packed[0][:, AT_LIFTED : AT_LIFTED + MICRO * SLOTS * D // shard]
+    lifted_rows = lifted_rows.reshape(devices, MICRO, SLOTS, devices, shard)
+    lifted_mine = lax.dynamic_index_in_dim(lifted_rows, section, 1, keepdims=False)
     lifted_mine = lax.dynamic_index_in_dim(
-        lifted_rows.reshape(devices, MICRO, SLOTS, shard), section, 1, keepdims=False
+        lifted_mine, lax.axis_index("row"), 2, keepdims=False
     ).reshape(devices * SLOTS, shard)
 
-    def summed(ffn, attn, mod, total):
-        ada_term = lax.dot_general(
+    def ada_term(mod):
+        return lax.dot_general(
             lifted_mine, flat(mod.held), (((0,), (0,)), ((), ())), preferred_element_type=f32
         )
-        return [attn.result(), ffn[0].result(), ffn[1].result(), ada_term, total]
-
-    total = totals[0].held
-    sums = (
-        summed(f1, one[0], mod1[0], total[:8]),
-        summed(f2, a2[0], mod2[0], total[8:]),
-    )
-    mine = [pick(pair) for pair in zip(*sums)]
-    other = [swap(pick_other(pair)) for pair in zip(*sums)]
-
-    def halves(number, axis):
-        mine_half, other_half = mine[number], other[number]
-        return jnp.concatenate(
-            [pick((mine_half, other_half)), pick_other((mine_half, other_half))], axis=axis
-        )
-
-    attn_total = halves(0, 1)
-    up_total = halves(1, 1)
-    down_total = halves(2, 0)
-    grad_w_ada = mine[3] + other[3]
-    small = mine[4] + other[4]
-
-    mod_own = pick((mod_low_one, mod_low_two))
-    mod_both = jnp.concatenate([pick((mod_own, mod_other)), pick_other((mod_own, mod_other))])
-    grad_lifted = mm_t(mod_both, ada)
-    grad_lifted = (grad_lifted + swap(grad_lifted)).reshape(MICRO * SLOTS, width, height, shard)
-    grad_lifted = grad_lifted.swapaxes(1, 2).reshape(MICRO, SLOTS, D)
+
+    ones = [a1, up1, down1, ada_term(mod_one), total.held[:8]]
+    twos = [a2, up2, down2, ada_term(mod_two), total.held[8:]]
+    sent_one, sent_two = divide(lock(*ones, *twos), 5, 5)
+    quads = [
+        (mine_one, mine_two, hand(one, 1), hand(two, 0))
+        for mine_one, mine_two, one, two in zip(ones, twos, sent_one, sent_two)
+    ]
+    (
+        g_query, g_key, g_value, g_gate, g_out, g_decay, g_up, g_down, g_ada,
+        g_b_ada, g_b_up, g_b_down, g_conv, g_b_decay,
+    ) = outputs(quads, shard, FF // devices // 2)
+
+    mod_both = jnp.where(
+        is_first,
+        jnp.concatenate([mod_low_one, mod_came_one]),
+        jnp.concatenate([mod_came_two, mod_low_two]),
+    )
+    grad_lifted = lifted_grads(mod_both, packed[0], vgd[0])
+    grad_lifted = (grad_lifted + swap(grad_lifted)).reshape(MICRO, SLOTS, D)
     _, pull_silu = jax.vjp(jax.nn.silu, conditions.astype(f32))
     (cond_grads,) = pull_silu(grad_lifted)
 
-    def assembled(pair, other):
-        mine = pick(pair)
-        return jnp.stack([pick((mine, other)), pick_other((mine, other))])
-
     return (
-        assembled(acts, acts_other)[None],
-        assembled((gx_one, gx_two), gx_other)[None],
+        both_micros(acts[0], acts[1], *acts_came)[None],
+        both_micros(gx_one, gx_two, gx_one_came, gx_two_came)[None],
         cond_grads,
-        grad_w_ada[None],
-        small[0:3].reshape(1, 6 * D),
-        attn_total[None, :, :D],
-        attn_total[None, :, D : 2 * D],
-        attn_total[None, :, 2 * D : 3 * D],
-        attn_total[None, :, 3 * D : 4 * D],
-        attn_total[None, :, 4 * D : 5 * D],
-        attn_total[None, :, 5 * D : 5 * D + HEADS],
-        small[7:8, :HEADS],
-        jnp.concatenate([small[5, D:], small[6]]).reshape(1, 3, D),
-        up_total[None],
-        small[3:5].reshape(1, FF),
-        down_total[None],
-        small[5:6, :D],
+        g_ada[None],
+        g_b_ada,
+        g_query[None],
+        g_key[None],
+        g_value[None],
+        g_gate[None],
+        g_out[None],
+        g_decay[None],
+        g_b_decay,
+        g_conv[None],
+        g_up[None],
+        g_b_up,
+        g_down.reshape(1, FF // devices, D),
+        g_b_down,
     )
 
 

time: 355 us -> 451 us (1.27)
  Pallas kernels: 109 us -> 181 us
  local copies, waits for them, and re-layouts: 21.2 us -> 46.6 us
  waiting for transfers between devices: 79.9 us -> 104 us
  starting transfers between devices: 70.8 us -> 91.7 us
  blocking collectives: 17.8 us -> 0 us
  other arithmetic: 29.4 us -> 13.5 us
  between operations: 15.6 us -> 2.59 us
    pallas_call x2 -> x15, Pallas kernels: 2.93 us -> 82.8 us  [the longest x2 73.7 us: both_micros(): pl.pallas_call(both_kernel, out_shape=jax.ShapeDtypeStruct((MICRO,) + one...]
    ppermute x0 -> x16, starting transfers between devices: none -> 29.3 us  [hand(): return lax.ppermute(values, 'section', [(source, 1 - source)])]
    ppermute x52 -> x48, waiting for transfers between devices: 78.1 us -> 99.4 us  [partner(): return lax.ppermute(values, 'row', [(i, i ^ 1 << bit) for i in range(size)])]
    all_gather x1 -> x0, blocking collectives: 17.8 us -> none  [on_device(): lax.all_gather(w_ada[0], 'row', axis_index_groups=groups(along_z), tiled=...]
    unnamed x105 -> x217, local copies, waits for them, and re-layouts: 8.72 us -> 24.2 us
    pallas_call x10, Pallas kernels: 105 us -> 97 us  [call(): pl.pallas_call(kernel, out_shape=[jax.ShapeDtypeStruct(shape, kind) for s...]
    ppermute x52 -> x48, starting transfers between devices: 66.6 us -> 58.7 us  [partner(): return lax.ppermute(values, 'row', [(i, i ^ 1 << bit) for i in range(size)])]
    add x26 -> x1, other arithmetic: 7.25 us -> 0.01 us  [on_device(): grad_lifted = (grad_lifted + swap(grad_lifted)).reshape(MICRO, SLOTS, D)]
  transfers between devices with their start and end apart: 73 -> 76, of which waited for: 23 -> 27; matrix products, arithmetic and copies ran while one was open for 13% -> 8% of each run, Pallas kernels for 20% -> 38%
where the time goes in v1:
time: 451 us; the launch traced here: 442 us
  Pallas kernels  181 us (40%)
  waiting for transfers between devices  104 us (23%)
  starting transfers between devices  91.7 us (20%)
  local copies, waits for them, and re-layouts  46.6 us (10%)
  other arithmetic  13.5 us (3%)
    ppermute x48, waiting for transfers between devices, partner(): return lax.ppermute(values, 'row', [(i, i ^ 1 << bit) for i in range(size)])  99.4 us
    pallas_call x10, Pallas kernels, call(): pl.pallas_call(kernel, out_shape=[jax.ShapeDtypeStruct(shape, kind) for s...  97 us
    pallas_call x2, Pallas kernels, both_micros(): pl.pallas_call(both_kernel, out_shape=jax.ShapeDtypeStruct((MICRO,) + one...  73.7 us
    ppermute x48, starting transfers between devices, partner(): return lax.ppermute(values, 'row', [(i, i ^ 1 << bit) for i in range(size)])  58.7 us
    ppermute x16, starting transfers between devices, hand(): return lax.ppermute(values, 'section', [(source, 1 - source)])  29.3 us
    unnamed x217, local copies, waits for them, and re-layouts  24.2 us
  transfers between devices with their start and end apart: 76, of which 27 were waited for; matrix products, arithmetic and copies ran while one was open for 8% of the time, Pallas kernels for 38%

profile of v1, /device:TPU:0, one launch (start us, length us, event | category | flops | bytes accessed | tf_op | source)
XLA Modules:
  0.0 442.0 jit_solution(11580194518833848614)
XLA Ops:
  8.0 4.1 collective-permute-start
  12.2 2.8 collective-permute-start.2
  15.0 13.5 %collective-permute-done.2 = bf16[1,1,1,1,96,384]{5,4,0,1,3,2:T(8,128)(2,1)S(1)} collective-permute-done((bf16[1,1,1,1,96,384]{5,4,0,1,3,2:T(8,128)(2,1)}, bf16[1,1,1,1,96,384]{5,4,0,1,3,2:T(8,128)(2,1)S(1)}, u32[]{:S(2)}, u32[]{:S(2)}) %collective-permute-start.2) | collective-permute-done | bytes 73760 | tf_op jit(solution)/shard_map/ppermute | solution.py:1148
  35.7 4.5 %collective-permute-done.4 = bf16[2,1,1,1,24,2176]{5,4,0,1,3,2:T(8,128)(2,1)S(1)} collective-permute-done((bf16[2,1,1,1,24,2176]{5,4,0,1,3,2:T(8,128)(2,1)S(1)}, bf16[2,1,1,1,24,2176]{5,4,0,1,3,2:T(8,128)(2,1)S(1)}, u32[]{:S(2)}, u32[]{:S(2)}) %collective-permute-start.4) | collective-permute-done | bytes 208928 | tf_op jit(solution)/shard_map/ppermute | solution.py:1148
  40.2 6.9 %collective-permute-done.3 = bf16[2,1,1,1,24,3840]{5,4,3,2,1,0:T(8,128)(2,1)S(1)} collective-permute-done((bf16[2,1,1,1,24,3840]{5,4,3,2,1,0:T(8,128)(2,1)S(1)}, bf16[2,1,1,1,24,3840]{5,4,3,2,1,0:T(8,128)(2,1)S(1)}, u32[]{:S(2)}, u32[]{:S(2)}) %collective-permute-start.3) | collective-permute-done | bytes 368672 | tf_op jit(solution)/shard_map/ppermute | solution.py:1148
  51.3 5.9 %collective-permute-done.8 = bf16[2,2,1,1,96,384]{5,4,0,1,3,2:T(8,128)(2,1)S(1)} collective-permute-done((bf16[2,2,1,1,96,384]{5,4,0,1,3,2:T(8,128)(2,1)S(1)}, bf16[2,2,1,1,96,384]{5,4,0,1,3,2:T(8,128)(2,1)S(1)}, u32[]{:S(2)}, u32[]{:S(2)}) %collective-permute-start.8) | collective-permute-done | bytes 294944 | tf_op jit(solution)/shard_map/ppermute | solution.py:1148
  57.2 7.1 %collective-permute-done.7 = bf16[2,2,1,1,24,2176]{5,4,0,1,3,2:T(8,128)(2,1)S(1)} collective-permute-done((bf16[2,2,1,1,24,2176]{5,4,0,1,3,2:T(8,128)(2,1)S(1)}, bf16[2,2,1,1,24,2176]{5,4,0,1,3,2:T(8,128)(2,1)S(1)}, u32[]{:S(2)}, u32[]{:S(2)}) %collective-permute-start.7) | collective-permute-done | bytes 417824 | tf_op jit(solution)/shard_map/ppermute | solution.py:1148
  69.6 28.6 %collective-permute-done.11 = bf16[2,2,2,1,96,384]{5,4,0,1,3,2:T(8,128)(2,1)S(1)} collective-permute-done((bf16[2,2,2,1,96,384]{5,4,0,1,3,2:T(8,128)(2,1)S(1)}, bf16[2,2,2,1,96,384]{5,4,0,1,3,2:T(8,128)(2,1)S(1)}, u32[]{:S(2)}, u32[]{:S(2)}) %collective-permute-start.11) | collective-permute-done | bytes 589856 | tf_op jit(solution)/shard_map/ppermute | solution.py:1148
  110.0 8.6 %shard_map.308 = (bf16[512,384]{1,0:T(8,128)(2,1)S(1)}, f32[512,1536]{1,0:T(8,128)}, f32[512,128]{1,0:T(8,128)S(1)}, f32[512,384]{1,0:T(8,128)S(1)}, f32[512,128...) custom-call(s32[2,1]{1,0:T(2,128)S(1)} %copy.66.refs_0_, ...), custom_call_target="tpu_custom_call" | custom-call | flops 8000000000 | bytes 4194304 | tf_op jit(solution)/shard_map/pallas_call | solution.py:707
  119.5 6.1 %shard_map.309 = (bf16[512,384]{1,0:T(8,128)(2,1)S(1)}, f32[512,384]{1,0:T(8,128)S(1)}, f32[512,384]{1,0:T(8,128)S(1)}) custom-call(s32[2,1]{1,0:T(2,128)S(1)} %copy.66.refs_0_, bf16[512,384]{1,0:T(8,128)(2,1)S(1)} %get-tuple-element.264.refs_1_.refs_13_, bf16[2,512,384]{2,1,0:T(8,128)(2,1)S(1)} %copy-done.32, bf16[384,3840]{1,0:T(8,128)(2,1)S(1)} %bitcast.172, ...), custom_call_target="tpu_custom_call" | custom-call | flops 5000000000 | bytes 4194304 | tf_op jit(solution)/shard_map/pallas_call | solution.py:707
  128.7 10.0 %shard_map.310 = (bf16[512,384]{1,0:T(8,128)(2,1)S(1)}, f32[512,1536]{1,0:T(8,128)}, f32[512,128]{1,0:T(8,128)S(1)}, f32[512,384]{1,0:T(8,128)S(1)}, f32[512,128...) custom-call(s32[2,1]{1,0:T(2,128)S(1)} %copy.66.refs_0_, ...), custom_call_target="tpu_custom_call" | custom-call | flops 8000000000 | bytes 4194304 | tf_op jit(solution)/shard_map/pallas_call | solution.py:707
  138.8 6.3 %shard_map.311 = (bf16[512,384]{1,0:T(8,128)(2,1)S(1)}, f32[512,384]{1,0:T(8,128)S(1)}, f32[512,384]{1,0:T(8,128)S(1)}) custom-call(s32[2,1]{1,0:T(2,128)S(1)} %copy.66.refs_0_, bf16[512,384]{1,0:T(8,128)(2,1)S(1)} %get-tuple-element.267.refs_1_.refs_13_, bf16[1,512,384]{2,1,0:T(8,128)(2,1)S(1)} %bitcast.204, bf16[384,3840]{1,0:T(8,128)(2,1)S(1)} %bitcast.175, ...), custom_call_target="tpu_custom_call" | custom-call | flops 5000000000 | bytes 4194304 | tf_op jit(solution)/shard_map/pallas_call | solution.py:707
  145.1 2.7 collective-permute-start.20
  147.9 12.5 %shard_map.312 = (f32[512,384]{1,0:T(8,128)S(1)}, bf16[512,384]{1,0:T(8,128)(2,1)S(1)}, f32[384,384]{1,0:T(8,128)S(1)}, f32[384,768]{1,0:T(8,128)S(1)}, bf16[384...) custom-call(s32[2,1]{1,0:T(2,128)S(1)} %copy.66.refs_0_, ...), custom_call_target="tpu_custom_call" | custom-call | flops 12000000000 | bytes 4194304 | tf_op jit(solution)/shard_map/pallas_call | solution.py:707
  163.5 15.4 %shard_map.313 = (bf16[512,1664]{1,0:T(8,128)(2,1)S(1)}, f32[384,1024]{1,0:T(8,128)S(1)}, bf16[384,1024]{1,0:T(8,128)(2,1)}, f32[8,384]{1,0:T(8,128)S(1)}) custom-call(s32[2,1]{1,0:T(2,128)S(1)} %copy.66.refs_0_, bf16[512,384]{1,0:T(8,128)(2,1)S(1)} %get-tuple-element.275.refs_1_, bf16[384,3840]{1,0:T(8,128)(2,1)} %bitcast.178, ...), custom_call_target="tpu_custom_call" | custom-call | flops 15000000512 | bytes 4194304 | tf_op jit(solution)/shard_map/pallas_call | solution.py:707
  185.0 5.4 %shard_map.315 = (f32[512,384]{1,0:T(8,128)S(1)}, bf16[512,384]{1,0:T(8,128)(2,1)S(1)}, bf16[8,2304]{1,0:T(8,128)(2,1)S(1)}, f32[8,768]{1,0:T(8,128)S(1)}) custom-call(s32[2,1]{1,0:T(2,128)S(1)} %copy.66.refs_0_, bf16[512,1664]{1,0:T(8,128)(2,1)S(1)} %copy-done.43, bf16[384,3840]{1,0:T(8,128)(2,1)} %bitcast.179, ...), custom_call_target="tpu_custom_call" | custom-call | flops 4000000000 | bytes 4194304 | tf_op jit(solution)/shard_map/pallas_call | solution.py:707
  200.7 12.7 %shard_map.317 = (f32[512,384]{1,0:T(8,128)S(1)}, bf16[512,384]{1,0:T(8,128)(2,1)S(1)}, f32[384,384]{1,0:T(8,128)S(1)}, f32[384,768]{1,0:T(8,128)S(1)}, bf16[384...) custom-call(s32[2,1]{1,0:T(2,128)S(1)} %copy.66.refs_0_, f32[4,2304]{1,0:T(4,128)S(1)} %copy-done.25, ...), custom_call_target="tpu_custom_call" | custom-call | flops 12000000000 | bytes 4194304 | tf_op jit(solution)/shard_map/pallas_call | solution.py:707
  233.9 14.6 %shard_map.320 = (bf16[512,1664]{1,0:T(8,128)(2,1)S(1)}, f32[384,1024]{1,0:T(8,128)S(1)}, bf16[384,1024]{1,0:T(8,128)(2,1)S(1)}, f32[8,384]{1,0:T(8,128)S(1)}) custom-call(s32[2,1]{1,0:T(2,128)S(1)} %copy.66.refs_0_, bf16[512,384]{1,0:T(8,128)(2,1)S(1)} %copy-done.73, bf16[384,3840]{1,0:T(8,128)(2,1)} %bitcast.182, ...), custom_call_target="tpu_custom_call" | custom-call | flops 15000000512 | bytes 4194304 | tf_op jit(solution)/shard_map/pallas_call | solution.py:707
  253.1 5.3 %shard_map.323 = (f32[512,384]{1,0:T(8,128)}, bf16[512,384]{1,0:T(8,128)(2,1)}, bf16[8,2304]{1,0:T(8,128)(2,1)S(1)}, f32[8,768]{1,0:T(8,128)S(1)}) custom-call(s32[2,1]{1,0:T(2,128)S(1)} %copy.66.refs_0_, bf16[512,1664]{1,0:T(8,128)(2,1)S(1)} %get-tuple-element.373.refs_1_, bf16[384,3840]{1,0:T(8,128)(2,1)} %bitcast.183, ...), custom_call_target="tpu_custom_call" | custom-call | flops 4000000000 | bytes 4194304 | tf_op jit(solution)/shard_map/pallas_call | solution.py:707
  260.6 4.6 %collective-permute-done.40 = bf16[4,24,768]{2,1,0:T(8,128)(2,1)S(1)} collective-permute-done((bf16[4,24,768]{2,1,0:T(8,128)(2,1)S(1)}, bf16[4,24,768]{2,1,0:T(8,128)(2,1)S(1)}, u32[]{:S(2)}, u32[]{:S(2)}) %collective-permute-start.40) | collective-permute-done | bytes 147488 | tf_op jit(solution)/shard_map/ppermute | solution.py:1148
  272.3 6.3 %collective-permute-done.46 = bf16[8,24,1024]{2,1,0:T(8,128)(2,1)S(1)} collective-permute-done((bf16[8,24,1024]{2,1,0:T(8,128)(2,1)S(1)}, bf16[8,24,1024]{2,1,0:T(8,128)(2,1)S(1)}, u32[]{:S(2)}, u32[]{:S(2)}) %collective-permute-start.46) | collective-permute-done | bytes 393248 | tf_op jit(solution)/shard_map/ppermute | solution.py:1148
  283.9 2.6 collective-permute-done.49
  295.9 3.4 collective-permute-start.58
  299.4 2.8 collective-permute-start.60
  303.2 2.9 collective-permute-start.57
  306.2 2.8 collective-permute-start.64
  313.3 3.1 collective-permute-done.62
  335.4 4.3 collective-permute-start.69
  350.6 25.0 %shard_map.314 = bf16[2,512,384]{2,1,0:T(8,128)(2,1)} custom-call(bf16[512,384]{1,0:T(8,128)(2,1)} %copy-done.13, bf16[512,384]{1,0:T(8,128)(2,1)} %copy-done.15, bf16[512,384]{1,0:T(8,128)(2,1)} %copy-done.79, bf16[512,384]{1,0:T(8,128)(2,1)} %copy-done.80), custom_call_target="tpu_custom_call" | custom-call | tf_op jit(solution)/shard_map/pallas_call | solution.py:1119
  378.3 3.0 collective-permute-start.67
  382.7 3.1 collective-permute-start.73
  386.4 48.8 %shard_map.324 = f32[2,512,384]{2,1,0:T(8,128)} custom-call(f32[512,384]{1,0:T(8,128)} %get-tuple-element.387.one, f32[512,384]{1,0:T(8,128)} %copy-done.2, f32[512,384]{1,0:T(8,128)} %collective-permute-done.42.one_came, f32[512,384]{1,0:T(8,128)} %copy-done.76), custom_call_target="tpu_custom_call" | custom-call | tf_op jit(solution)/shard_map/pallas_call | solution.py:1119
  (427 shorter events, 153.8 us)
Async XLA Ops:
  8.0 20.5 %collective-permute-start = (bf16[1,1,1,1,24,3840]{5,4,3,2,1,0:T(8,128)(2,1)}, bf16[1,1,1,1,24,3840]{5,4,3,2,1,0:T(8,128)(2,1)S(1)}, u32[]{:S(2)}, u32[]{:S(2)}) collective-permute-start(bf16[1,1,1,1,24,3840]{5,4,3,2,1,0:T(8,128)(2,1)} %bitcast.249), channel_id=1, source_target_pairs={{0,8},{1,9},{2,10},{3,11},{4,12},{5,13},{6,14},{7,15},{8,0},{9,1},... | collective-permute-start | bytes 552968 | tf_op jit(solution)/shard_map/ppermute | solution.py:1148
  12.1 16.4 %collective-permute-start.1 = (bf16[1,1,1,1,24,2176]{5,4,0,1,3,2:T(8,128)(2,1)}, bf16[1,1,1,1,24,2176]{5,4,0,1,3,2:T(8,128)(2,1)S(1)}, u32[]{:S(2)}, u32[]{:S(2)}) collective-permute-start(bf16[1,1,1,1,24,2176]{5,4,0,1,3,2:T(8,128)(2,1)} %bitcast.254), channel_id=1, source_target_pairs={{0,8},{1,9},{2,10},{3,11},{4,12},{5,13},{6,14},{7,15},{8,0},{9,1},... | collective-permute-start | bytes 313352 | tf_op jit(solution)/shard_map/ppermute | solution.py:1148
  12.2 16.4 %collective-permute-start.2 = (bf16[1,1,1,1,96,384]{5,4,0,1,3,2:T(8,128)(2,1)}, bf16[1,1,1,1,96,384]{5,4,0,1,3,2:T(8,128)(2,1)S(1)}, u32[]{:S(2)}, u32[]{:S(2)}) collective-permute-start(bf16[1,1,1,1,96,384]{5,4,0,1,3,2:T(8,128)(2,1)} %bitcast.258), channel_id=1, source_target_pairs={{0,8},{1,9},{2,10},{3,11},{4,12},{5,13},{6,14},{7,15},{8,0},{9,1},... | collective-permute-start | bytes 221192 | tf_op jit(solution)/shard_map/ppermute | solution.py:1148
  49.0 17.3 %collective-permute-start.6 = (bf16[2,2,1,1,24,3840]{5,4,3,2,1,0:T(8,128)(2,1)S(1)}, bf16[2,2,1,1,24,3840]{5,4,3,2,1,0:T(8,128)(2,1)S(1)}, u32[]{:S(2)}, u32[]{:S(2)}) collective-permute-start(bf16[2,2,1,1,24,3840]{5,4,3,2,1,0:T(8,128)(2,1)S(1)} %maximum_select_fusion.6), channel_id=1, source_target_pairs={{0,1},{1,0},{2,3},{3,2},{4,5},{5,4},{6,7},{7,6},{8,9},{9,8},{10,11... | collective-permute-start | bytes 2211848 | tf_op jit(solution)/shard_map/ppermute | solution.py:1148
  66.5 32.2 %collective-permute-start.9 = (bf16[2,2,1,2,24,3840]{5,4,3,2,1,0:T(8,128)(2,1)S(1)}, bf16[2,2,1,2,24,3840]{5,4,3,2,1,0:T(8,128)(2,1)S(1)}, u32[]{:S(2)}, u32[]{:S(2)}) collective-permute-start(bf16[2,2,1,2,24,3840]{5,4,3,2,1,0:T(8,128)(2,1)S(1)} %maximum_select_fusion.2), channel_id=1, source_target_pairs={{0,2},{1,3},{2,0},{3,1},{4,6},{5,7},{6,4},{7,5},{8,10},{9,11},{10,... | collective-permute-start | bytes 4423688 | tf_op jit(solution)/shard_map/ppermute | solution.py:1148
  67.3 30.9 %collective-permute-start.10 = (bf16[2,2,2,1,24,2176]{5,4,0,1,3,2:T(8,128)(2,1)S(1)}, bf16[2,2,2,1,24,2176]{5,4,0,1,3,2:T(8,128)(2,1)S(1)}, u32[]{:S(2)}, u32[]{:S(2)}) collective-permute-start(bf16[2,2,2,1,24,2176]{5,4,0,1,3,2:T(8,128)(2,1)S(1)} %maximum_select_fusion.4), channel_id=1, source_target_pairs={{0,1},{1,0},{2,3},{3,2},{4,5},{5,4},{6,7},{7,6},{8,9},{9,8},{10,11... | collective-permute-start | bytes 2506760 | tf_op jit(solution)/shard_map/ppermute | solution.py:1148
  69.0 29.2 %collective-permute-start.11 = (bf16[2,2,2,1,96,384]{5,4,0,1,3,2:T(8,128)(2,1)S(1)}, bf16[2,2,2,1,96,384]{5,4,0,1,3,2:T(8,128)(2,1)S(1)}, u32[]{:S(2)}, u32[]{:S(2)}) collective-permute-start(bf16[2,2,2,1,96,384]{5,4,0,1,3,2:T(8,128)(2,1)S(1)} %maximum_select_fusion.7), channel_id=1, source_target_pairs={{0,1},{1,0},{2,3},{3,2},{4,5},{5,4},{6,7},{7,6},{8,9},{9,8},{10,11... | collective-permute-start | bytes 1769480 | tf_op jit(solution)/shard_map/ppermute | solution.py:1148
  102.7 16.8 %collective-permute-start.16 = (bf16[1536,384]{1,0:T(8,128)(2,1)}, bf16[1536,384]{1,0:T(8,128)(2,1)}, u32[]{:S(2)}, u32[]{:S(2)}) collective-permute-start(bf16[1536,384]{1,0:T(8,128)(2,1)} %bitcast.34.refs_11_), channel_id=1, source_target_pairs={{0,16},{16,0},{1,17},{17,1},{2,18},{18,2},{3,19},{19,3},{4,20},{20... | collective-permute-start | bytes 3538952 | tf_op jit(solution)/shard_map/ppermute | solution.py:1129
  127.4 52.7 %collective-permute-start.19 = (bf16[512,384]{1,0:T(8,128)(2,1)S(1)}, bf16[512,384]{1,0:T(8,128)(2,1)S(1)}, u32[]{:S(2)}, u32[]{:S(2)}) collective-permute-start(bf16[512,384]{1,0:T(8,128)(2,1)S(1)} %get-tuple-element.266.one), channel_id=1, source_target_pairs={{16,0},{17,1},{18,2},{19,3},{20,4},{21,5},{22,6},{23,7},{24,8},{25... | collective-permute-start | bytes 1179656 | tf_op jit(solution)/shard_map/ppermute | solution.py:1133
  145.1 35.0 %collective-permute-start.20 = (bf16[512,384]{1,0:T(8,128)(2,1)S(1)}, bf16[512,384]{1,0:T(8,128)(2,1)S(1)}, u32[]{:S(2)}, u32[]{:S(2)}) collective-permute-start(bf16[512,384]{1,0:T(8,128)(2,1)S(1)} %get-tuple-element.268.two), channel_id=1, source_target_pairs={{0,16},{1,17},{2,18},{3,19},{4,20},{5,21},{6,22},{7,23},{8,24},{9,... | collective-permute-start | bytes 1179656 | tf_op jit(solution)/shard_map/ppermute | solution.py:1133
  162.1 18.0 %collective-permute-start.17 = (bf16[16,24,768]{2,1,0:T(8,128)(2,1)S(1)}, bf16[16,24,768]{2,1,0:T(8,128)(2,1)S(1)}, u32[]{:S(2)}, u32[]{:S(2)}) collective-permute-start(bf16[16,24,768]{2,1,0:T(8,128)(2,1)S(1)} %bitcast.238), channel_id=1, source_target_pairs={{0,16},{16,0},{1,17},{17,1},{2,18},{18,2},{3,19},{19,3},{4,20},{20... | collective-permute-start | bytes 1769480 | tf_op jit(solution)/shard_map/ppermute | solution.py:1129
  162.2 18.8 %collective-permute-start.18 = (bf16[16,48,384]{2,1,0:T(8,128)(2,1)S(1)}, bf16[16,48,384]{2,1,0:T(8,128)(2,1)S(1)}, u32[]{:S(2)}, u32[]{:S(2)}) collective-permute-start(bf16[16,48,384]{2,1,0:T(8,128)(2,1)S(1)} %fusion.1), channel_id=1, source_target_pairs={{0,16},{16,0},{1,17},{17,1},{2,18},{18,2},{3,19},{19,3},{4,20},{20... | collective-permute-start | bytes 1769480 | tf_op jit(solution)/shard_map/ppermute | solution.py:1129
  195.2 22.3 %collective-permute-start.25 = (bf16[1,1,1,1,2,2304]{5,4,3,2,1,0:T(2,128)(2,1)S(1)}, bf16[1,1,1,1,2,2304]{5,4,3,2,1,0:T(2,128)(2,1)S(1)}, u32[]{:S(2)}, u32[]{:S(2)}) collective-permute-start(bf16[1,1,1,1,2,2304]{5,4,3,2,1,0:T(2,128)(2,1)S(1)} %bitcast.262), channel_id=1, source_target_pairs={{0,1},{1,0},{2,3},{3,2},{4,5},{5,4},{6,7},{7,6},{8,9},{9,8},{10,11... | collective-permute-start | bytes 27656 | tf_op jit(solution)/shard_map/ppermute | solution.py:1148
  196.7 20.8 %collective-permute-start.22 = (bf16[8,24,768]{2,1,0:T(8,128)(2,1)S(1)}, bf16[8,24,768]{2,1,0:T(8,128)(2,1)S(1)}, u32[]{:S(2)}, u32[]{:S(2)}) collective-permute-start(bf16[8,24,768]{2,1,0:T(8,128)(2,1)S(1)} %get-tuple-element.316), channel_id=1, source_target_pairs={{0,1},{1,0},{2,3},{3,2},{4,5},{5,4},{6,7},{7,6},{8,9},{9,8},{10,11... | collective-permute-start | bytes 884744 | tf_op jit(solution)/shard_map/ppermute | solution.py:1148
  197.2 21.0 %collective-permute-start.23 = (bf16[8,48,384]{2,1,0:T(8,128)(2,1)S(1)}, bf16[8,48,384]{2,1,0:T(8,128)(2,1)S(1)}, u32[]{:S(2)}, u32[]{:S(2)}) collective-permute-start(bf16[8,48,384]{2,1,0:T(8,128)(2,1)S(1)} %get-tuple-element.317), channel_id=1, source_target_pairs={{0,1},{1,0},{2,3},{3,2},{4,5},{5,4},{6,7},{7,6},{8,9},{9,8},{10,11... | collective-permute-start | bytes 884744 | tf_op jit(solution)/shard_map/ppermute | solution.py:1148
  198.8 21.8 %collective-permute-start.24 = (bf16[8,24,1024]{2,1,0:T(8,128)(2,1)S(1)}, bf16[8,24,1024]{2,1,0:T(8,128)(2,1)S(1)}, u32[]{:S(2)}, u32[]{:S(2)}) collective-permute-start(bf16[8,24,1024]{2,1,0:T(8,128)(2,1)S(1)} %get-tuple-element.318), channel_id=1, source_target_pairs={{0,1},{1,0},{2,3},{3,2},{4,5},{5,4},{6,7},{7,6},{8,9},{9,8},{10,11... | collective-permute-start | bytes 1179656 | tf_op jit(solution)/shard_map/ppermute | solution.py:1148
  199.3 21.3 %collective-permute-start.26 = (f32[512,384]{1,0:T(8,128)S(1)}, f32[512,384]{1,0:T(8,128)S(1)}, u32[]{:S(2)}, u32[]{:S(2)}) collective-permute-start(f32[512,384]{1,0:T(8,128)S(1)} %get-tuple-element.320.two), channel_id=1, source_target_pairs={{0,16},{1,17},{2,18},{3,19},{4,20},{5,21},{6,22},{7,23},{8,24},{9,... | collective-permute-start | bytes 2359304 | tf_op jit(solution)/shard_map/ppermute | solution.py:1133
  228.6 19.8 %collective-permute-start.29 = (bf16[4,24,768]{2,1,0:T(8,128)(2,1)S(1)}, bf16[4,24,768]{2,1,0:T(8,128)(2,1)S(1)}, u32[]{:S(2)}, u32[]{:S(2)}) collective-permute-start(bf16[4,24,768]{2,1,0:T(8,128)(2,1)S(1)} %get-tuple-element.349), channel_id=1, source_target_pairs={{0,2},{1,3},{2,0},{3,1},{4,6},{5,7},{6,4},{7,5},{8,10},{9,11},{10,... | collective-permute-start | bytes 442376 | tf_op jit(solution)/shard_map/ppermute | solution.py:1148
  229.7 18.7 %collective-permute-start.30 = (bf16[4,48,384]{2,1,0:T(8,128)(2,1)S(1)}, bf16[4,48,384]{2,1,0:T(8,128)(2,1)S(1)}, u32[]{:S(2)}, u32[]{:S(2)}) collective-permute-start(bf16[4,48,384]{2,1,0:T(8,128)(2,1)S(1)} %get-tuple-element.350), channel_id=1, source_target_pairs={{0,2},{1,3},{2,0},{3,1},{4,6},{5,7},{6,4},{7,5},{8,10},{9,11},{10,... | collective-permute-start | bytes 442376 | tf_op jit(solution)/shard_map/ppermute | solution.py:1148
  230.7 17.7 %collective-permute-start.31 = (bf16[4,24,1024]{2,1,0:T(8,128)(2,1)S(1)}, bf16[4,24,1024]{2,1,0:T(8,128)(2,1)S(1)}, u32[]{:S(2)}, u32[]{:S(2)}) collective-permute-start(bf16[4,24,1024]{2,1,0:T(8,128)(2,1)S(1)} %get-tuple-element.351), channel_id=1, source_target_pairs={{0,2},{1,3},{2,0},{3,1},{4,6},{5,7},{6,4},{7,5},{8,10},{9,11},{10,... | collective-permute-start | bytes 589832 | tf_op jit(solution)/shard_map/ppermute | solution.py:1148
  231.8 16.7 %collective-permute-start.33 = (bf16[8,24,768]{2,1,0:T(8,128)(2,1)S(1)}, bf16[8,24,768]{2,1,0:T(8,128)(2,1)S(1)}, u32[]{:S(2)}, u32[]{:S(2)}) collective-permute-start(bf16[8,24,768]{2,1,0:T(8,128)(2,1)S(1)} %get-tuple-element.353), channel_id=1, source_target_pairs={{0,1},{1,0},{2,3},{3,2},{4,5},{5,4},{6,7},{7,6},{8,9},{9,8},{10,11... | collective-permute-start | bytes 884744 | tf_op jit(solution)/shard_map/ppermute | solution.py:1148
  248.8 18.0 %collective-permute-start.35 = (bf16[16,24,1024]{2,1,0:T(8,128)(2,1)S(1)}, bf16[16,24,1024]{2,1,0:T(8,128)(2,1)S(1)}, u32[]{:S(2)}, u32[]{:S(2)}) collective-permute-start(bf16[16,24,1024]{2,1,0:T(8,128)(2,1)S(1)} %bitcast.237), channel_id=1, source_target_pairs={{0,16},{16,0},{1,17},{17,1},{2,18},{18,2},{3,19},{19,3},{4,20},{20... | collective-permute-start | bytes 2359304 | tf_op jit(solution)/shard_map/ppermute | solution.py:1129
  312.0 64.9 %collective-permute-start.42 = (f32[512,384]{1,0:T(8,128)}, f32[512,384]{1,0:T(8,128)}, u32[]{:S(2)}, u32[]{:S(2)}) collective-permute-start(f32[512,384]{1,0:T(8,128)} %get-tuple-element.387.one), channel_id=1, source_target_pairs={{16,0},{17,1},{18,2},{19,3},{20,4},{21,5},{22,6},{23,7},{24,8},{25... | collective-permute-start | bytes 2359304 | tf_op jit(solution)/shard_map/ppermute | solution.py:1133
  334.1 44.2 %collective-permute-start.68 = (f32[24,768]{1,0:T(8,128)}, f32[24,768]{1,0:T(8,128)}, u32[]{:S(2)}, u32[]{:S(2)}) collective-permute-start(f32[24,768]{1,0:T(8,128)} %get-tuple-element.463.refs_4_), channel_id=1, source_target_pairs={{16,0},{17,1},{18,2},{19,3},{20,4},{21,5},{22,6},{23,7},{24,8},{25... | collective-permute-start | bytes 221192 | tf_op jit(solution)/shard_map/ppermute | solution.py:1133
  335.4 46.0 %collective-permute-start.69 = (f32[24,768]{1,0:T(8,128)S(1)}, f32[24,768]{1,0:T(8,128)}, u32[]{:S(2)}, u32[]{:S(2)}) collective-permute-start(f32[24,768]{1,0:T(8,128)S(1)} %get-tuple-element.464.refs_5_), channel_id=1, source_target_pairs={{0,16},{1,17},{2,18},{3,19},{4,20},{5,21},{6,22},{7,23},{8,24},{9,... | collective-permute-start | bytes 221192 | tf_op jit(solution)/shard_map/ppermute | solution.py:1133
  339.6 43.1 %collective-permute-start.70 = (f32[48,384]{1,0:T(8,128)}, f32[48,384]{1,0:T(8,128)}, u32[]{:S(2)}, u32[]{:S(2)}) collective-permute-start(f32[48,384]{1,0:T(8,128)} %get-tuple-element.465.refs_8_), channel_id=1, source_target_pairs={{16,0},{17,1},{18,2},{19,3},{20,4},{21,5},{22,6},{23,7},{24,8},{25... | collective-permute-start | bytes 221192 | tf_op jit(solution)/shard_map/ppermute | solution.py:1133
  348.6 27.1 %collective-permute-start.75 = (f32[8,768]{1,0:T(8,128)}, f32[8,768]{1,0:T(8,128)S(1)}, u32[]{:S(2)}, u32[]{:S(2)}) collective-permute-start(f32[8,768]{1,0:T(8,128)} %get-tuple-element.470.refs_17_), channel_id=1, source_target_pairs={{0,16},{1,17},{2,18},{3,19},{4,20},{5,21},{6,22},{7,23},{8,24},{9,... | collective-permute-start | bytes 73736 | tf_op jit(solution)/shard_map/ppermute | solution.py:1133
  375.6 59.5 %collective-permute-start.71 = (f32[48,384]{1,0:T(8,128)S(1)}, f32[48,384]{1,0:T(8,128)S(1)}, u32[]{:S(2)}, u32[]{:S(2)}) collective-permute-start(f32[48,384]{1,0:T(8,128)S(1)} %copy-done.84), channel_id=1, source_target_pairs={{0,16},{1,17},{2,18},{3,19},{4,20},{5,21},{6,22},{7,23},{8,24},{9,... | collective-permute-start | bytes 221192 | tf_op jit(solution)/shard_map/ppermute | solution.py:1133
  377.0 58.2 %collective-permute-start.66 = (f32[24,1024]{1,0:T(8,128)S(1)}, f32[24,1024]{1,0:T(8,128)S(1)}, u32[]{:S(2)}, u32[]{:S(2)}) collective-permute-start(f32[24,1024]{1,0:T(8,128)S(1)} %copy-done.82), channel_id=1, source_target_pairs={{16,0},{17,1},{18,2},{19,3},{20,4},{21,5},{22,6},{23,7},{24,8},{25... | collective-permute-start | bytes 294920 | tf_op jit(solution)/shard_map/ppermute | solution.py:1133
  378.3 56.9 %collective-permute-start.67 = (f32[24,1024]{1,0:T(8,128)S(1)}, f32[24,1024]{1,0:T(8,128)S(1)}, u32[]{:S(2)}, u32[]{:S(2)}) collective-permute-start(f32[24,1024]{1,0:T(8,128)S(1)} %copy-done.81), channel_id=1, source_target_pairs={{0,16},{1,17},{2,18},{3,19},{4,20},{5,21},{6,22},{7,23},{8,24},{9,... | collective-permute-start | bytes 294920 | tf_op jit(solution)/shard_map/ppermute | solution.py:1133
  381.4 53.9 %collective-permute-start.72 = (f32[24,2304]{1,0:T(8,128)S(1)}, f32[24,2304]{1,0:T(8,128)S(1)}, u32[]{:S(2)}, u32[]{:S(2)}) collective-permute-start(f32[24,2304]{1,0:T(8,128)S(1)} %fusion.21.refs_12_), channel_id=1, source_target_pairs={{16,0},{17,1},{18,2},{19,3},{20,4},{21,5},{22,6},{23,7},{24,8},{25... | collective-permute-start | bytes 663560 | tf_op jit(solution)/shard_map/ppermute | solution.py:1133
  382.7 52.6 %collective-permute-start.73 = (f32[24,2304]{1,0:T(8,128)S(1)}, f32[24,2304]{1,0:T(8,128)S(1)}, u32[]{:S(2)}, u32[]{:S(2)}) collective-permute-start(f32[24,2304]{1,0:T(8,128)S(1)} %copy-done.74), channel_id=1, source_target_pairs={{0,16},{1,17},{2,18},{3,19},{4,20},{5,21},{6,22},{7,23},{8,24},{9,... | collective-permute-start | bytes 663560 | tf_op jit(solution)/shard_map/ppermute | solution.py:1133
  (149 other events, 1398.8 us)
